TPU v7x, 256 devices: a whole 4x4x8 slice. The times are simulated.
256 devices in a mesh: group: 8 (over z_hi, core), tp: 32 (over x, y, z_lo).
Axes of the slice: x: 4, y: 4, z: 8 (z_hi: 4, z_lo: 2; z = z_hi * 2 + z_lo), core: 2. Of those that a mesh axis runs over, the one named last changes fastest.
Arguments:
- prefill_x: bfloat16 [1024, 16384], P('group', 'tp'), may hold values from -6 to 6
- prefill_gate: bfloat16 [1024, 16384], P('group', 'tp'), may hold values from -6 to 6
- lengths: int32 [8, 8], P('group'), may hold values from 1 to 64, 128 in all within a row
- routes: int32 [64, 1], replicated, may hold values from 0 to 7; in each aligned block of 8 rows (0 to 7, 8 to 15, ...) at most 2 rows name the same one
- decode_x: bfloat16 [4, 256, 16384], P(None, 'group', 'tp'), may hold values from -6 to 6
- decode_gate: bfloat16 [4, 256, 16384], P(None, 'group', 'tp'), may hold values from -6 to 6
- cached_state: float32 [256, 16, 16384], P('group', None, 'tp'), may hold values from -4 to 4
- xproj_weight: bfloat16 [16384, 544], P('tp'), may hold values from -0.046875 to 0.046875
- dt_weight: bfloat16 [512, 16384], P(None, 'tp'), may hold values from -0.25 to 0.25
- dt_bias: float32 [16384], P('tp'), may hold values from -3 to -1
- a_log: float32 [16, 16384], P(None, 'tp'), may hold values from 0 to 2.77
- skip_gain: float32 [16384], P('tp'), may hold values from 0.5 to 1.5
Outputs:
- prefill_out: bfloat16 [1024, 16384], P('group', 'tp')
- decode_out: bfloat16 [4, 256, 16384], P(None, 'group', 'tp')
Inputs may be any that keep to these rules, and one draw needn't show every extreme that they name: `routes`: in each aligned block of 8 rows (the requests of one group) no decode group is named more than 2 times. `lengths`: each group's row sums to 128; its largest entry is 64.
All inputs are finite; a program needn't handle non-finite values.
Results may differ from a plain program's by a relative error of at most 0.0051.
Values sent between devices are 32-bit elements; how exact they have to be, the bound alone decides.
No kernel may reach another device: no remote copies, remote signals or barrier semaphores. Data moves between devices by JAX's collectives and lax.ppermute only.
A program may use at most 64 MiB of HBM per device.

v0:
```python
import jax
import jax.numpy as jnp
from jax import lax
from jax.sharding import PartitionSpec as P


def project_columns(inputs, xproj_weight):
    return lax.dot_general(
        xproj_weight, inputs, (((0,), (1,)), ((), ())), preferred_element_type=jnp.float32
    )


def mixer_terms(projected, dt_weight, dt_bias, state_width):
    low_rank = dt_weight.shape[0]
    low_part = projected[:low_rank].astype(jnp.bfloat16)
    step_size = jax.nn.softplus(
        lax.dot_general(
            low_part, dt_weight, (((0,), (0,)), ((), ())), preferred_element_type=jnp.float32
        )
        + dt_bias
    )
    vectors = jnp.transpose(projected[low_rank:])
    return (step_size, vectors[:, :state_width], vectors[:, state_width:])


def combine(earlier, latter):
    return (earlier[0] * latter[0], latter[0] * earlier[1] + latter[1])


def gated_output(hidden, readout, values, skip_gain, gate_rows):
    mixed = jnp.sum(readout[:, :, None] * hidden, axis=1)
    return ((mixed + skip_gain * values) * jax.nn.silu(gate_rows.astype(jnp.float32))).astype(
        jnp.bfloat16
    )


def local(
    prefill_x,
    prefill_gate,
    lengths,
    routes,
    decode_x,
    decode_gate,
    cached_state,
    xproj_weight,
    dt_weight,
    dt_bias,
    a_log,
    skip_gain,
):
    state_width = a_log.shape[0]
    channels = prefill_x.shape[1]
    tokens = prefill_x.shape[0]
    row_count = cached_state.shape[0]
    step_count = decode_x.shape[0]
    group_index = lax.axis_index("group")
    rates = -jnp.exp(a_log)
    prefill_part = project_columns(prefill_x, xproj_weight)
    decode_part = project_columns(decode_x.reshape(step_count * row_count, channels), xproj_weight)
    prefill_proj = lax.psum(prefill_part, "tp")
    decode_proj = lax.psum(decode_part, "tp")
    step_size, inject, readout = mixer_terms(prefill_proj, dt_weight, dt_bias, state_width)
    lengths_here = lengths[0]
    request_end = jnp.cumsum(lengths_here) - 1
    request_start = request_end - lengths_here + 1
    block_size = min(256, tokens)
    carried = jnp.zeros((state_width, channels), jnp.float32)
    position = 0 + jnp.arange(block_size, dtype=jnp.int32)
    first_token = jnp.any(position[:, None] == request_start[None, :], axis=1)
    survive = jnp.where(first_token, jnp.float32(0.0), jnp.float32(1.0))
    values = prefill_x.astype(jnp.float32)
    damping = survive[:, None, None] * jnp.exp(step_size[:, None, :] * rates[None])
    forcing = step_size[:, None, :] * inject[0:block_size, :, None] * values[:, None, :]
    prefix_damping, prefix_forcing = lax.associative_scan(combine, (damping, forcing), axis=0)
    hidden = prefix_damping * carried[None] + prefix_forcing
    pieces = gated_output(hidden, readout, values, skip_gain, prefill_gate)
    selector = (request_end[:, None] == position[None, :]).astype(jnp.float32)
    final_states = jnp.einsum("kt,tse->kse", selector, hidden, precision=lax.Precision.HIGHEST)
    flat_routes = routes[:, 0]
    total_requests = flat_routes.shape[0]
    ordering = jnp.arange(total_requests, dtype=jnp.int32)
    same_dest = flat_routes[:, None] == flat_routes[None, :]
    slot_index = jnp.sum(
        ((ordering[:, None] > ordering[None, :]) & same_dest).astype(jnp.int32), axis=1
    )
    destinations = flat_routes * row_count + slot_index
    row_ids = group_index * row_count + jnp.arange(row_count, dtype=jnp.int32)
    state_pool = lax.all_gather(final_states, "group", axis=0, tiled=True)
    matches = row_ids[:, None] == destinations[None, :]
    arrived = jnp.any(matches, axis=1)
    source = jnp.argmax(matches.astype(jnp.int32), axis=1)
    hidden = jnp.where(arrived[:, None, None], state_pool[source], cached_state)
    step_all, inject_all, readout_all = mixer_terms(decode_proj, dt_weight, dt_bias, state_width)
    step_all = step_all.reshape(step_count, row_count, channels)
    inject_all = inject_all.reshape(step_count, row_count, state_width)
    readout_all = readout_all.reshape(step_count, row_count, state_width)
    results = []
    for step_index in range(step_count):
        step_now = step_all[step_index]
        values = decode_x[step_index].astype(jnp.float32)
        hidden = (
            jnp.exp(step_now[:, None, :] * rates[None]) * hidden
            + step_now[:, None, :] * inject_all[step_index][:, :, None] * values[:, None, :]
        )
        results.append(
            gated_output(
                hidden, readout_all[step_index], values, skip_gain, decode_gate[step_index]
            )
        )
    decode_out = jnp.stack(results)
    return (pieces, decode_out)


def solution(mesh):
    placed = (
        P("group", "tp"),
        P("group", "tp"),
        P("group", None),
        P(),
        P(None, "group", "tp"),
        P(None, "group", "tp"),
        P("group", None, "tp"),
        P("tp", None),
        P(None, "tp"),
        P("tp"),
        P(None, "tp"),
        P("tp"),
    )
    return jax.shard_map(
        local,
        mesh=mesh,
        in_specs=placed,
        out_specs=(P("group", "tp"), P(None, "group", "tp")),
        check_vma=False,
    )
```

profile of v0, /device:TPU:1, one launch (start us, length us, event | category | flops | bytes accessed | tf_op | source)
XLA Modules:
  0.0 608.3 jit_solution(11258771613676732315)
XLA Ops:
  12.5 283.4 %all-reduce.31.cloned.1.call-done = (f32[544,128]{1,0:T(8,128)}, f32[544,128]{1,0:T(8,128)}) async-done(((f32[544,128]{1,0:T(8,128)}, f32[544,128]{1,0:T(8,128)}), (f32[544,128]{1,0:T(8,128)}, f32[544,128]{1,0:T(8,128)})) %all-reduce.31.cloned.1.call-update) | async-done | bytes 557072 | tf_op jit(solution)/shard_map/psum | solution.py:60
  302.4 10.0 %slice.336 = f32[63,16,512]{2,0,1:T(8,128)} slice(f32[128,16,512]{2,0,1:T(8,128)} %copy-done.2), slice={[2:128:2], [0:16:1], [0:512:1]} | slice | bytes 4128768 | tf_op jit(solution)/shard_map/slice | solution.py:74
  312.4 9.9 %slice.307 = f32[64,16,512]{2,0,1:T(8,128)} slice(f32[128,16,512]{2,0,1:T(8,128)} %copy-done.2), slice={[1:128:2], [0:16:1], [0:512:1]} | slice | bytes 4194304 | tf_op jit(solution)/shard_map/slice | solution.py:74
  322.2 9.8 %slice.306 = f32[64,16,512]{2,0,1:T(8,128)} slice(f32[128,16,512]{2,0,1:T(8,128)} %copy-done.2), slice={[0:127:2], [0:16:1], [0:512:1]} | slice | bytes 4194304 | tf_op jit(solution)/shard_map/slice | solution.py:74
  333.0 10.0 %slice.369 = f32[63,16,512]{2,0,1:T(8,128)} slice(f32[128,16,512]{2,0,1:T(8,128)} %get-tuple-element.37), slice={[2:128:2], [0:16:1], [0:512:1]} | slice | bytes 4128768 | tf_op jit(solution)/shard_map/slice | solution.py:74
  343.0 9.9 %slice.340 = f32[64,16,512]{2,0,1:T(8,128)} slice(f32[128,16,512]{2,0,1:T(8,128)} %get-tuple-element.37), slice={[1:128:2], [0:16:1], [0:512:1]} | slice | bytes 4194304 | tf_op jit(solution)/shard_map/slice | solution.py:74
  352.9 9.8 %slice.339 = f32[64,16,512]{2,0,1:T(8,128)} slice(f32[128,16,512]{2,0,1:T(8,128)} %get-tuple-element.37), slice={[0:127:2], [0:16:1], [0:512:1]} | slice | bytes 4194304 | tf_op jit(solution)/shard_map/slice | solution.py:74
  362.6 4.5 fusion.47
  368.6 5.4 slice.334
  374.0 5.4 slice.310
  379.4 5.4 slice.309
  384.8 2.9 slice.367
  387.7 2.8 slice.343
  390.6 2.9 slice.342
  393.4 2.7 fusion.48
  417.2 6.2 %pad.94 = f32[32,16,512]{2,0,1:T(8,128)S(1)} pad(f32[16,16,512]{2,0,1:T(8,128)} %pad_maximum_fusion.4, f32[]{:T(128)} %constant.36.clone.1), padding=0_1_1x0_0_0x0_0_0 | pad | bytes 1572868 | tf_op jit(solution)/shard_map/pad | solution.py:74
  423.4 6.1 pad.95
  429.5 6.1 pad.109
  443.4 7.1 %pad.110 = f32[64,16,512]{2,0,1:T(8,128)S(1)} pad(f32[32,16,512]{2,0,1:T(8,128)} %pad_maximum_fusion.3, f32[]{:T(128)} %constant.36.clone.1), padding=0_1_1x0_0_0x0_0_0 | pad | bytes 3145732 | tf_op jit(solution)/shard_map/pad | solution.py:74
  452.9 10.5 %pad.96 = f32[64,16,512]{2,0,1:T(8,128)} pad(f32[32,16,512]{2,0,1:T(8,128)} %pad_maximum_fusion.2, f32[]{:T(128)} %constant.36.clone.1), padding=0_1_1x0_0_0x0_0_0 | pad | bytes 3145732 | tf_op jit(solution)/shard_map/pad | solution.py:74
  463.4 10.5 %pad.97 = f32[64,16,512]{2,0,1:T(8,128)} pad(f32[32,16,512]{2,0,1:T(8,128)} %add.266, f32[]{:T(128)} %constant.36.clone.1), padding=1_0_1x0_0_0x0_0_0 | pad | bytes 3145732 | tf_op jit(solution)/shard_map/pad | solution.py:74
  473.8 10.4 %pad.111 = f32[64,16,512]{2,0,1:T(8,128)} pad(f32[32,16,512]{2,0,1:T(8,128)} %add.284, f32[]{:T(128)} %constant.36.clone.1), padding=1_0_1x0_0_0x0_0_0 | pad | bytes 3145732 | tf_op jit(solution)/shard_map/pad | solution.py:74
  484.3 3.6 add.286
  491.5 2.9 add_multiply_fusion.1
  494.7 8.0 %pad.112 = f32[128,16,512]{2,0,1:T(8,128)} pad(f32[64,16,512]{2,0,1:T(8,128)S(1)} %pad_maximum_fusion.1, f32[]{:T(128)} %constant.36.clone.1), padding=0_1_1x0_0_0x0_0_0 | pad | bytes 6291460 | tf_op jit(solution)/shard_map/pad | solution.py:74
  504.6 8.0 %pad.98 = f32[128,16,512]{2,0,1:T(8,128)} pad(f32[64,16,512]{2,0,1:T(8,128)S(1)} %pad_maximum_fusion, f32[]{:T(128)} %constant.36.clone.1), padding=0_1_1x0_0_0x0_0_0 | pad | bytes 6291460 | tf_op jit(solution)/shard_map/pad | solution.py:74
  512.6 12.1 %pad.99 = f32[128,16,512]{2,0,1:T(8,128)} pad(f32[64,16,512]{2,0,1:T(8,128)} %add.267, f32[]{:T(128)} %constant.36.clone.1), padding=1_0_1x0_0_0x0_0_0 | pad | bytes 6291460 | tf_op jit(solution)/shard_map/pad | solution.py:74
  524.7 8.0 %pad.113 = f32[128,16,512]{2,0,1:T(8,128)} pad(f32[64,16,512]{2,0,1:T(8,128)S(1)} %copy-done.9, f32[]{:T(128)} %constant.36.clone.1), padding=1_0_1x0_0_0x0_0_0 | pad | bytes 6291460 | tf_op jit(solution)/shard_map/pad | solution.py:74
  532.7 6.4 %multiply_reduce_fusion = (f32[128,512]{1,0:T(8,128)S(1)}, f32[128,16,512]{2,0,1:T(8,128)S(1)}) fusion(f32[128,16]{0,1:T(8,128)S(1)} %get-tuple-element.65, f32[128,16,512]{2,0,1:T(8,128)} %pad.112, f32[128,16,512]{2,0,1:T(8,128)} %pad.113, f32[128,16,512]{2,0,1:T(8,128)} %pad.98, f32[128,16,512]{2,0,1:T(8,128)} %pad.99), kind=kLoop, calls=%fused_computation.1 | loop fusion | flops 6225920 | bytes 21241856 | tf_op jit(solution)/shard_map/reduce_sum | solution.py:31
  550.3 42.4 %all-gather.2.cloned.1.call-done = f32[64,16,512]{2,0,1:T(8,128)} async-done(((f32[8,16,512]{2,0,1:T(8,128)}), f32[64,16,512]{2,0,1:T(8,128)}) %all-gather.2.cloned.1.call-update) | async-done | bytes 2097168 | tf_op jit(solution)/shard_map/all_gather | solution.py:88
  592.6 2.8 copy.25
  597.4 3.3 multiply_reduce_fusion.2
  (189 shorter events, 64.5 us)
Async XLA Ops:
  7.2 5.2 copy-start.21
  7.2 4.9 copy-start.33
  7.2 5.3 copy-start.28
  7.2 289.4 %copy-start.29 = (f32[512]{0:T(512)S(1)}, f32[512]{0:T(512)}, u32[]{:S(2)}) copy-start(f32[512]{0:T(512)} %param.21) | copy-start | bytes 6148
  7.2 289.4 %copy-start.15 = (bf16[512,512]{1,0:T(8,128)(2,1)S(1)}, bf16[512,512]{1,0:T(8,128)(2,1)}, u32[]{:S(2)}) copy-start(bf16[512,512]{1,0:T(8,128)(2,1)} %param.20) | copy-start | bytes 1572868
  7.2 288.7 %all-reduce.31.cloned.1.call-start = ((), (), s32[]{:S(2)}) async-start(), calls=%async_computation.1 | async-start | bytes 1114112 | tf_op jit(solution)/shard_map/psum | solution.py:60
  12.1 580.6 %all-gather.2.cloned.1.call-start = ((), (), s32[]{:S(2)}) async-start(), calls=%async_computation | async-start | bytes 2359296 | tf_op jit(solution)/shard_map/all_gather | solution.py:88
  300.4 2.0 copy-start.2
  367.2 1.4 copy-start.6
  399.4 3.2 copy-start.17
  415.3 8.1 %copy-start.14 = (f32[16,16,512]{2,0,1:T(8,128)S(1)}, f32[16,16,512]{2,0,1:T(8,128)}, u32[]{:S(2)}) copy-start(f32[16,16,512]{2,0,1:T(8,128)} %add.265) | copy-start | bytes 1572868
  435.6 2.5 copy-start.7
  438.1 1.9 copy-start.12
  438.1 2.2 copy-start.13
  484.3 3.6 copy-start.3
  484.3 3.6 copy-start.4
  487.8 1.9 copy-start.5
  487.8 3.0 copy-start.10
  487.8 3.6 copy-start.11
  512.6 12.1 %copy-start.9 = (f32[64,16,512]{2,0,1:T(8,128)S(1)}, f32[64,16,512]{2,0,1:T(8,128)}, u32[]{:S(2)}) copy-start(f32[64,16,512]{2,0,1:T(8,128)} %add.286) | copy-start | bytes 6291460
  539.1 2.3 copy-start.34
  539.1 4.5 copy-start.22
  539.1 9.4 %copy-start.16 = (bf16[512,512]{1,0:T(8,128)(2,1)S(1)}, bf16[512,512]{1,0:T(8,128)(2,1)}, u32[]{:S(2)}) copy-start(bf16[512,512]{1,0:T(8,128)(2,1)} %param.20) | copy-start | bytes 1572868
  539.1 9.3 %copy-start.23 = (f32[544,128]{1,0:T(8,128)S(1)}, f32[544,128]{1,0:T(8,128)}, u32[]{:S(2)}) copy-start(f32[544,128]{1,0:T(8,128)} %get-tuple-element.9) | copy-start | bytes 835588
  539.1 9.3 %copy-start.30 = (f32[512]{0:T(512)S(1)}, f32[512]{0:T(512)}, u32[]{:S(2)}) copy-start(f32[512]{0:T(512)} %param.21) | copy-start | bytes 6148
  541.3 8.2 %copy-start.26 = (bf16[128,512]{1,0:T(8,128)(2,1)S(1)}, bf16[128,512]{1,0:T(8,128)(2,1)}, u32[]{:S(2)}) copy-start(bf16[128,512]{1,0:T(8,128)(2,1)} %param.13) | copy-start | bytes 393220
  541.3 8.2 %copy-start.31 = (f32[512]{0:T(512)S(1)}, f32[512]{0:T(512)}, u32[]{:S(2)}) copy-start(f32[512]{0:T(512)} %param.23) | copy-start | bytes 6148
  595.4 1.9 copy-start.24
  595.5 1.9 copy-start.25
  595.5 6.0 copy-start.1
  597.3 3.3 copy-start.27
  597.3 3.3 copy-start.32
  (5 other events, 5.7 us)
Sparse Core Ops, SparseCore 0:
  12.2 283.6 all-reduce.30
  541.4 51.1 all-gather.1
where the time goes:
time: 614 us; the launch traced here: 608 us
  waiting for transfers between devices  326 us (53%)
  local copies, waits for them, and re-layouts  211 us (34%)
  other arithmetic  48.6 us (8%)
  between operations  14.8 us (2%)
  matrix products  7.69 us (1%)
    psum x1, waiting for transfers between devices, local(): prefill_proj = lax.psum(prefill_part, 'tp')  283 us
    slice x44, local copies, waits for them, and re-layouts, local(): lax.associative_scan(combine, (damping, forcing), axis=0)  96.9 us
    pad x24, local copies, waits for them, and re-layouts, local(): lax.associative_scan(combine, (damping, forcing), axis=0)  95.4 us
    all_gather x1, waiting for transfers between devices, local(): state_pool = lax.all_gather(final_states, 'group', axis=0, tiled=True)  42.4 us
    mul x12, other arithmetic, combine(): return (earlier[0] * latter[0], latter[0] * earlier[1] + latter[1])  14.9 us
  transfers between devices with their start and end apart: 2, of which 2 were waited for; matrix products, arithmetic and copies ran while one was open for 2% of the time, Pallas kernels for 0%

commit v1 on v0

v1 whole, which is shorter than its diff:
```python
import functools

import jax
import jax.numpy as jnp
from jax import lax
from jax.experimental import pallas as pl
from jax.experimental.pallas import tpu as pltpu
from jax.sharding import PartitionSpec as P

LOG2E = 1.4426950408889634
FAR = 1e30
LANES = 128
VMEM_LIMIT = 40 * 1024 * 1024

VMEM = pl.BlockSpec(memory_space=pltpu.VMEM)
SMEM = pl.BlockSpec(memory_space=pltpu.SMEM)


def params():
    return pltpu.CompilerParams(vmem_limit_bytes=VMEM_LIMIT)


def softplus(v):
    return jnp.maximum(v, 0.0) + jnp.log1p(jnp.exp(-jnp.abs(v)))


def silu(v):
    return v / (1.0 + jnp.exp(-v))


def project_kernel(prefill_ref, decode_ref, weight_ref, out_ref):
    tokens = prefill_ref.shape[0]
    weight = weight_ref[...]
    half = out_ref.shape[0] // 2
    first = jnp.dot(prefill_ref[...], weight, preferred_element_type=jnp.float32)
    out_ref[:half] = first.reshape(half, tokens // half, -1)
    second = jnp.dot(decode_ref[...], weight, preferred_element_type=jnp.float32)
    out_ref[half:] = second.reshape(half, tokens // half, -1)


def total_kernel(parts_ref, out_ref):
    total = jnp.sum(parts_ref[...], axis=0)
    out_ref[...] = jnp.broadcast_to(total[None], out_ref.shape)


def step_sizes(proj, weight_ref, bias_ref):
    rank = weight_ref.shape[0]
    low = proj[:, :rank].astype(jnp.bfloat16)
    return softplus(
        jnp.dot(low, weight_ref[...], preferred_element_type=jnp.float32) + bias_ref[...]
    )


def advance(hidden, rates_ref, size_row, forcing_row, inject, readout):
    mixed = []
    for tile in range(len(hidden)):
        cols = slice(tile * LANES, (tile + 1) * LANES)
        damping = jnp.exp2(size_row[:, cols] * rates_ref[:, cols])
        hidden[tile] = damping * hidden[tile] + forcing_row[:, cols] * inject
        mixed.append(jnp.sum(readout * hidden[tile], axis=0, keepdims=True))
    return jnp.concatenate(mixed, axis=1)


def prefill_kernel(
    lengths_ref, routes_ref, proj_ref, x_ref, gate_ref, weight_ref, bias_ref, alog_ref, skip_ref,
    out_ref, send_ref,
    size_ref, force_ref, mixed_ref, vec_ref, rates_ref, hist_ref,
):
    tokens, channels = x_ref.shape
    width = alog_ref.shape[0]
    requests = lengths_ref.shape[1]
    rank = weight_ref.shape[0]
    group = lax.axis_index("group")
    proj = proj_ref[...].reshape(tokens, -1)
    size = step_sizes(proj, weight_ref, bias_ref)
    values = x_ref[...].astype(jnp.float32)
    force_ref[...] = size * values
    position = lax.broadcasted_iota(jnp.int32, (tokens, LANES), 0)
    first = position == 0
    begin = jnp.int32(0)
    ends = []
    for k in range(requests):
        first = first | (position == begin)
        begin = begin + lengths_ref[0, k]
        ends.append(begin - 1)
    reset = jnp.where(first, jnp.float32(FAR), jnp.float32(0.0))
    for tile in range(channels // LANES):
        cols = slice(tile * LANES, (tile + 1) * LANES)
        size_ref[:, cols] = size[:, cols] + reset
    vec_ref[...] = jnp.transpose(proj[:, rank:])
    rates_ref[...] = -LOG2E * jnp.exp(alog_ref[...])

    def block(b, hidden):
        base = pl.multiple_of(b * 8, 8)
        vectors = pltpu.roll(vec_ref[...], tokens - base, axis=1)
        sizes = size_ref[pl.ds(base, 8), :]
        forces = force_ref[pl.ds(base, 8), :]
        hidden = list(hidden)
        rows = []
        for i in range(8):
            inject = jnp.broadcast_to(vectors[:width, i : i + 1], (width, LANES))
            readout = jnp.broadcast_to(vectors[width:, i : i + 1], (width, LANES))
            rows.append(
                advance(
                    hidden, rates_ref, sizes[i : i + 1], forces[i : i + 1], inject, readout
                )
            )
            for tile in range(len(hidden)):
                hist_ref[base + i, :, tile * LANES : (tile + 1) * LANES] = hidden[tile]
        mixed_ref[pl.ds(base, 8), :] = jnp.concatenate(rows, axis=0)
        return tuple(hidden)

    zero = jnp.zeros((width, LANES), jnp.float32)
    lax.fori_loop(0, tokens // 8, block, (zero,) * (channels // LANES))
    out_ref[...] = (
        (mixed_ref[...] + skip_ref[...] * values) * silu(gate_ref[...].astype(jnp.float32))
    ).astype(out_ref.dtype)
    dests = [routes_ref[group * requests + k, 0] for k in range(requests)]
    for k in range(requests):
        lane = jnp.int32(0)
        for j in range(k):
            lane = lane + (dests[j] == dests[k]).astype(jnp.int32)
        send_ref[dests[k], lane] = hist_ref[ends[k]]


def decode_kernel(
    routes_ref, proj_ref, recv_ref, state_ref, x_ref, gate_ref, weight_ref, bias_ref, alog_ref,
    skip_ref,
    out_ref,
    size_ref, force_ref, mixed_ref, vec_ref, rates_ref, start_ref,
):
    total, channels = x_ref.shape
    rows, width = state_ref.shape[:2]
    steps = total // rows
    groups, cap = recv_ref.shape[:2]
    requests = routes_ref.shape[0] // groups
    rank = weight_ref.shape[0]
    me = lax.axis_index("group")
    proj = proj_ref[...].reshape(total, -1)
    size = step_sizes(proj, weight_ref, bias_ref)
    values = x_ref[...].astype(jnp.float32)
    size_ref[...] = size
    force_ref[...] = size * values
    vec_ref[...] = jnp.transpose(proj[:, rank:])
    rates_ref[...] = -LOG2E * jnp.exp(alog_ref[...])
    start_ref[...] = state_ref[...]
    slot = jnp.int32(0)
    for g in range(groups):
        count = jnp.int32(0)
        for k in range(requests):
            count = count + (routes_ref[g * requests + k, 0] == me).astype(jnp.int32)
        for c in range(cap):

            @pl.when(count > c)
            def _(g=g, c=c, slot=slot):
                start_ref[slot + c] = recv_ref[g, c]

        slot = slot + count

    def block(b, carry):
        base = pl.multiple_of(b * 8, 8)
        vectors, sizes, forces = [], [], []
        for s in range(steps):
            at = pl.multiple_of(s * rows + base, 8)
            vectors.append(pltpu.roll(vec_ref[...], total - at, axis=1))
            sizes.append(size_ref[pl.ds(at, 8), :])
            forces.append(force_ref[pl.ds(at, 8), :])
        results = [[] for _ in range(steps)]
        for i in range(8):
            hidden = [
                start_ref[base + i, :, tile * LANES : (tile + 1) * LANES]
                for tile in range(channels // LANES)
            ]
            for s in range(steps):
                inject = jnp.broadcast_to(vectors[s][:width, i : i + 1], (width, LANES))
                readout = jnp.broadcast_to(vectors[s][width:, i : i + 1], (width, LANES))
                results[s].append(
                    advance(
                        hidden, rates_ref, sizes[s][i : i + 1], forces[s][i : i + 1], inject, readout
                    )
                )
        for s in range(steps):
            at = pl.multiple_of(s * rows + base, 8)
            mixed_ref[pl.ds(at, 8), :] = jnp.concatenate(results[s], axis=0)
        return carry

    lax.fori_loop(0, rows // 8, block, 0)
    out_ref[...] = (
        (mixed_ref[...] + skip_ref[...] * values) * silu(gate_ref[...].astype(jnp.float32))
    ).astype(out_ref.dtype)


def local(
    prefill_x, prefill_gate, lengths, routes, decode_x, decode_gate, cached_state, xproj_weight,
    dt_weight, dt_bias, a_log, skip_gain, *, ranks, groups, cap,
):
    tokens, channels = prefill_x.shape
    steps, rows, _ = decode_x.shape
    width = a_log.shape[0]
    columns = xproj_weight.shape[1]
    decode_rows = steps * rows
    decode_flat = decode_x.reshape(decode_rows, channels)
    gate_flat = decode_gate.reshape(decode_rows, channels)
    bias = dt_bias.reshape(1, channels)
    skip = skip_gain.reshape(1, channels)
    per = (tokens + decode_rows) // ranks
    chunked = jax.ShapeDtypeStruct((ranks, per, columns), jnp.float32)

    partial = pl.pallas_call(
        project_kernel, out_shape=chunked, in_specs=[VMEM] * 3, out_specs=VMEM,
        compiler_params=params(), name="project",
    )(prefill_x, decode_flat, xproj_weight)
    parts = lax.all_to_all(partial, "tp", 0, 0)
    copies = pl.pallas_call(
        total_kernel, out_shape=chunked, in_specs=[VMEM], out_specs=VMEM,
        compiler_params=params(), name="total",
    )(parts)
    proj = lax.all_to_all(copies, "tp", 0, 0)

    def part(index):
        return pl.BlockSpec((ranks // 2, per, columns), lambda i: (index, 0, 0))

    def f32(*shape):
        return pltpu.VMEM(shape, jnp.float32)

    prefill_out, send = pl.pallas_call(
        prefill_kernel,
        grid=(1,),
        out_shape=(
            jax.ShapeDtypeStruct((tokens, channels), jnp.bfloat16),
            jax.ShapeDtypeStruct((groups, cap, width, channels), jnp.float32),
        ),
        in_specs=[SMEM, SMEM, part(0)] + [VMEM] * 6,
        out_specs=(VMEM, VMEM),
        scratch_shapes=[
            f32(tokens, channels), f32(tokens, channels), f32(tokens, channels),
            f32(2 * width, tokens), f32(width, channels), f32(tokens, width, channels),
        ],
        compiler_params=params(), name="prefill",
    )(lengths, routes, proj, prefill_x, prefill_gate, dt_weight, bias, a_log, skip)
    recv = lax.all_to_all(send, "group", 0, 0)
    decode_out = pl.pallas_call(
        decode_kernel,
        grid=(1,),
        out_shape=jax.ShapeDtypeStruct((decode_rows, channels), jnp.bfloat16),
        in_specs=[SMEM, part(1)] + [VMEM] * 8,
        out_specs=VMEM,
        scratch_shapes=[
            f32(decode_rows, channels), f32(decode_rows, channels), f32(decode_rows, channels),
            f32(2 * width, decode_rows), f32(width, channels), f32(rows, width, channels),
        ],
        compiler_params=params(), name="decode",
    )(routes, proj, recv, cached_state, decode_flat, gate_flat, dt_weight, bias, a_log, skip)
    return prefill_out, decode_out.reshape(steps, rows, channels)


def solution(mesh):
    placed = (
        P("group", "tp"), P("group", "tp"), P("group", None), P(), P(None, "group", "tp"),
        P(None, "group", "tp"), P("group", None, "tp"), P("tp", None), P(None, "tp"), P("tp"),
        P(None, "tp"), P("tp"),
    )
    body = functools.partial(local, ranks=mesh.shape["tp"], groups=mesh.shape["group"], cap=2)
    return jax.shard_map(
        body, mesh=mesh, in_specs=placed, out_specs=(P("group", "tp"), P(None, "group", "tp")),
        check_vma=False,
    )
```

time: 614 us -> 77.7 us (0.13)
  waiting for transfers between devices: 326 us -> 11.5 us
  local copies, waits for them, and re-layouts: 211 us -> 1.54 us
  other arithmetic: 48.6 us -> 0 us
  blocking collectives: 0 us -> 48.3 us
  between operations: 14.8 us -> 0.75 us
  Pallas kernels: 0 us -> 11.3 us
  matrix products: 7.69 us -> 0 us
    psum x1 -> x0, waiting for transfers between devices: 283 us -> none  [local(): prefill_proj = lax.psum(prefill_part, 'tp')]
    slice x55 -> x0, local copies, waits for them, and re-layouts: 102 us -> none  [the longest x44 96.9 us: local(): lax.associative_scan(combine, (damping, forcing), axis=0)]
    pad x24 -> x0, local copies, waits for them, and re-layouts: 95.4 us -> none  [local(): lax.associative_scan(combine, (damping, forcing), axis=0)]
    all_to_all x0 -> x2, blocking collectives: none -> 48.3 us  [the longest x1 26.9 us: local(): recv = lax.all_to_all(send, 'group', 0, 0)]
    all_gather x1 -> x0, waiting for transfers between devices: 42.4 us -> none  [local(): state_pool = lax.all_gather(final_states, 'group', axis=0, tiled=True)]
    mul x13 -> x0, other arithmetic: 17.3 us -> none  [the longest x12 14.9 us: combine(): return (earlier[0] * latter[0], latter[0] * earlier[1] + latter[1])]
    all_to_all x0 -> x1, waiting for transfers between devices: none -> 11.5 us  [local(): proj = lax.all_to_all(copies, 'tp', 0, 0)]
    pallas_call x0 -> x4, Pallas kernels: none -> 11.3 us  [the longest x1 5.67 us: local(): pl.pallas_call(prefill_kernel, grid=(1,), out_shape=(jax.ShapeDtypeStruct...]
  transfers between devices with their start and end apart: 2 -> 1, of which waited for: 2 -> 1; matrix products, arithmetic and copies ran while one was open for 2% -> 0% of each run, Pallas kernels for 0% -> 0%
where the time goes in v1:
time: 77.7 us; the launch traced here: 77.4 us
  blocking collectives  48.3 us (62%)
  waiting for transfers between devices  11.5 us (15%)
  Pallas kernels  11.3 us (15%)
  starting transfers between devices  4.04 us (5%)
  local copies, waits for them, and re-layouts  1.54 us (2%)
    all_to_all x1, blocking collectives, local(): recv = lax.all_to_all(send, 'group', 0, 0)  26.9 us
    all_to_all x1, blocking collectives, local(): parts = lax.all_to_all(partial, 'tp', 0, 0)  21.4 us
    all_to_all x1, waiting for transfers between devices, local(): proj = lax.all_to_all(copies, 'tp', 0, 0)  11.5 us
    pallas_call x1, Pallas kernels, local(): pl.pallas_call(prefill_kernel, grid=(1,), out_shape=(jax.ShapeDtypeStruct...  5.67 us
    pallas_call x1, Pallas kernels, local(): pl.pallas_call(decode_kernel, grid=(1,), out_shape=jax.ShapeDtypeStruct((...  4.29 us
    all_to_all x1, starting transfers between devices, local(): proj = lax.all_to_all(copies, 'tp', 0, 0)  4.04 us
  transfers between devices with their start and end apart: 1, of which 1 were waited for; matrix products, arithmetic and copies ran while one was open for 0% of the time, Pallas kernels for 0%

profile of v1, /device:TPU:1, one launch (start us, length us, event | category | flops | bytes accessed | tf_op | source)
XLA Modules:
  0.0 77.4 jit_solution(5779154486720546277)
XLA Ops:
  0.6 0.0 copy-start.3
  0.6 0.0 copy-start.2
  0.6 1.4 %copy.14.weight_ref = bf16[512,544]{1,0:T(8,128)(2,1)S(1)} copy(bf16[512,544]{0,1:T(8,128)(2,1)} %param.19) | data formatting | bytes 1114112 | tf_op args[7]
  2.0 0.0 copy-done.3
  2.1 0.0 copy-done.2
  2.1 0.4 project.1
  2.4 21.4 %all_to_all.15.parts_ref = f32[32,8,544]{2,1,0:T(8,128)S(1)} all-to-all(f32[32,8,544]{2,1,0:T(8,128)S(1)} %project.1), channel_id=1, replica_groups=mesh['group'=8,'tp'=32] {'tp'}, dimensions={0} | all-to-all | bytes 1114112 | tf_op jit(solution)/shard_map/all_to_all | solution.py:213
  23.9 0.9 %total.1 = f32[32,8,544]{2,1,0:T(8,128)} custom-call(f32[32,8,544]{2,1,0:T(8,128)S(1)} %all_to_all.15.parts_ref), custom_call_target="tpu_custom_call" | custom-call | tf_op jit(solution)/shard_map/total/pallas_call | solution.py:214
  24.8 0.0 copy-start.10
  24.8 0.0 copy-start
  24.8 0.0 copy-start.6
  24.8 0.0 copy-start.9
  24.8 4.0 %all-to-all-start.1 = ((f32[32,8,544]{2,1,0:T(8,128)}), f32[32,8,544]{2,1,0:T(8,128)S(1)}, u32[]{:S(2)}, u32[]{:S(2)}) async-start(f32[32,8,544]{2,1,0:T(8,128)} %total.1), calls=%async_computation.1 | async-start | bytes 1310720 | tf_op jit(solution)/shard_map/all_to_all | solution.py:218
  28.9 0.0 copy-done.10
  28.9 0.0 copy-start.4
  28.9 0.0 copy-start.8
  28.9 0.1 copy.15.routes_ref
  29.0 0.0 copy-start.7
  29.0 11.5 %all-to-all-done.1.proj_ref = f32[32,8,544]{2,1,0:T(8,128)S(1)} async-done(((f32[32,8,544]{2,1,0:T(8,128)}), f32[32,8,544]{2,1,0:T(8,128)S(1)}, u32[]{:S(2)}, u32[]{:S(2)}) %all-to-all-start.1) | async-done | bytes 557088 | tf_op jit(solution)/shard_map/all_to_all | solution.py:218
  40.5 0.0 copy-done
  40.5 0.0 copy-done.6
  40.5 0.0 copy-done.9
  40.5 0.0 copy-done.4
  40.5 0.0 copy-done.8
  40.5 0.0 copy-done.7
  40.5 0.0 copy-start.1
  40.5 5.7 %prefill.1 = (bf16[128,512]{1,0:T(8,128)(2,1)}, f32[8,2,16,512]{3,2,1,0:T(8,128)S(1)}) custom-call(s32[1,8]{1,0:T(1,128)S(1)} %copy-done.9, s32[64,1]{1,0:T(8,128)S(1)} %copy.15.routes_ref, f32[32,8,544]{2,1,0:T(8,128)S(1)} %all-to-all-done.1.proj_ref, bf16[128,512]{1,0:T(8,128)(2,1)S(1)} %copy-done.3, bf16[128,512]{1,0:T(8,128)(2,1)S(1)} %copy-done.6, ...), custom_call_target="tpu_custom_call" | custom-call | tf_op jit(solution)/shard_map/prefill/pallas_call | solution.py:226
  46.2 0.0 copy-start.5
  46.2 26.9 %all_to_all.16.recv_ref = f32[8,2,16,512]{3,2,1,0:T(8,128)S(1)} all-to-all(f32[8,2,16,512]{3,2,1,0:T(8,128)S(1)} %get-tuple-element.5), channel_id=1, replica_groups=mesh['group'=8,'tp'=32] {'group'}, dimensions={0} | all-to-all | bytes 1048576 | tf_op jit(solution)/shard_map/all_to_all | solution.py:241
  73.1 0.0 copy-done.1
  73.1 0.0 copy-done.5
  73.1 4.3 %decode.1 = bf16[128,512]{1,0:T(8,128)(2,1)} custom-call(s32[64,1]{1,0:T(8,128)S(1)} %copy.15.routes_ref, f32[32,8,544]{2,1,0:T(8,128)S(1)} %all-to-all-done.1.proj_ref, f32[8,2,16,512]{3,2,1,0:T(8,128)S(1)} %all_to_all.16.recv_ref, f32[32,16,512]{2,1,0:T(8,128)S(1)} %copy-done.1, bf16[128,512]{1,0:T(8,128)(2,1)S(1)} %bitcast.6, ...), custom_call_target="tpu_custom_call" | custom-call | tf_op jit(solution)/shard_map/decode/pallas_call | solution.py:242
Async XLA Ops:
  0.6 1.4 %copy-start.3 = (bf16[128,512]{1,0:T(8,128)(2,1)S(1)}, bf16[128,512]{1,0:T(8,128)(2,1)}, u32[]{:S(2)}) copy-start(bf16[128,512]{1,0:T(8,128)(2,1)} %x_ref.1) | copy-start | bytes 393220
  0.6 1.4 %copy-start.2 = (bf16[4,32,512]{2,1,0:T(8,128)(2,1)S(1)}, bf16[4,32,512]{2,1,0:T(8,128)(2,1)}, u32[]{:S(2)}) copy-start(bf16[4,32,512]{2,1,0:T(8,128)(2,1)} %param.16) | copy-start | bytes 393220
  24.8 4.1 %copy-start.10 = (s32[64,1]{0,1:T(1,128)S(1)}, s32[64,1]{0,1:T(1,128)}, u32[]{:S(2)}) copy-start(s32[64,1]{0,1:T(1,128)} %param.15) | copy-start | bytes 772
  24.8 15.7 %copy-start = (bf16[512,512]{1,0:T(8,128)(2,1)S(1)}, bf16[512,512]{1,0:T(8,128)(2,1)}, u32[]{:S(2)}) copy-start(bf16[512,512]{1,0:T(8,128)(2,1)} %weight_ref.4) | copy-start | bytes 1572868
  24.8 15.7 %copy-start.6 = (bf16[128,512]{1,0:T(8,128)(2,1)S(1)}, bf16[128,512]{1,0:T(8,128)(2,1)}, u32[]{:S(2)}) copy-start(bf16[128,512]{1,0:T(8,128)(2,1)} %gate_ref.1) | copy-start | bytes 393220
  24.8 15.7 %copy-start.9 = (s32[1,8]{1,0:T(1,128)S(1)}, s32[1,8]{1,0:T(1,128)}, u32[]{:S(2)}) copy-start(s32[1,8]{1,0:T(1,128)} %lengths_ref.1) | copy-start | bytes 100
  24.8 15.7 %all-to-all-start.1 = ((f32[32,8,544]{2,1,0:T(8,128)}), f32[32,8,544]{2,1,0:T(8,128)S(1)}, u32[]{:S(2)}, u32[]{:S(2)}) async-start(f32[32,8,544]{2,1,0:T(8,128)} %total.1), calls=%async_computation.1 | async-start | bytes 1310720 | tf_op jit(solution)/shard_map/all_to_all | solution.py:218
  28.9 11.6 %copy-start.4 = (f32[16,512]{1,0:T(8,128)S(1)}, f32[16,512]{1,0:T(8,128)}, u32[]{:S(2)}) copy-start(f32[16,512]{1,0:T(8,128)} %alog_ref.3) | copy-start | bytes 98308
  28.9 11.6 %copy-start.8 = (f32[512]{0:T(512)S(1)}, f32[512]{0:T(512)}, u32[]{:S(2)}) copy-start(f32[512]{0:T(512)} %param.23) | copy-start | bytes 6148
  29.0 11.5 %copy-start.7 = (f32[512]{0:T(512)S(1)}, f32[512]{0:T(512)}, u32[]{:S(2)}) copy-start(f32[512]{0:T(512)} %param.21) | copy-start | bytes 6148
  40.5 32.6 %copy-start.1 = (f32[32,16,512]{2,1,0:T(8,128)S(1)}, f32[32,16,512]{2,1,0:T(8,128)}, u32[]{:S(2)}) copy-start(f32[32,16,512]{2,1,0:T(8,128)} %state_ref.1) | copy-start | bytes 3145732
  46.2 26.9 %copy-start.5 = (bf16[4,32,512]{2,1,0:T(8,128)(2,1)S(1)}, bf16[4,32,512]{2,1,0:T(8,128)(2,1)}, u32[]{:S(2)}) copy-start(bf16[4,32,512]{2,1,0:T(8,128)(2,1)} %param.17) | copy-start | bytes 393220

commit v2 on v1

v2 whole, which is shorter than its diff:
```python
import functools

import jax
import jax.numpy as jnp
from jax import lax
from jax.experimental import pallas as pl
from jax.experimental.pallas import tpu as pltpu
from jax.sharding import PartitionSpec as P

LOG2E = 1.4426950408889634
FAR = 1e30
LANES = 128
CAP = 2

VMEM = pl.BlockSpec(memory_space=pltpu.VMEM)
SMEM = pl.BlockSpec(memory_space=pltpu.SMEM)
ANY = pl.BlockSpec(memory_space=pl.ANY)


def call(kernel, name, out_shape, in_specs, out_specs=VMEM, scratch=(), mib=16, flops=0):
    return pl.pallas_call(
        kernel,
        grid=(1,),
        out_shape=out_shape,
        in_specs=in_specs,
        out_specs=out_specs,
        scratch_shapes=scratch,
        compiler_params=pltpu.CompilerParams(vmem_limit_bytes=mib << 20),
        cost_estimate=pl.CostEstimate(flops=flops, bytes_accessed=1 << 20, transcendentals=0),
        name=name,
    )


def f32(*shape):
    return pltpu.VMEM(shape, jnp.float32)


def bf16(*shape):
    return pltpu.VMEM(shape, jnp.bfloat16)


def struct(shape, dtype=jnp.float32):
    return jax.ShapeDtypeStruct(shape, dtype)


def stay(*arrays):
    return tuple(pltpu.with_memory_space_constraint(a, pltpu.HBM) for a in arrays)


def fetch(sources, targets, sems):
    copies = [
        pltpu.make_async_copy(a, b, sems.at[i]) for i, (a, b) in enumerate(zip(sources, targets))
    ]
    for copy in copies:
        copy.start()
    return copies


def softplus(v):
    return jnp.maximum(v, 0.0) + jnp.log1p(jnp.exp(-jnp.abs(v)))


def silu(v):
    return v / (1.0 + jnp.exp(-v))


def tiles_of(channels):
    return [slice(t, t + LANES) for t in range(0, channels, LANES)]


def project_kernel(
    weight_hbm, prefill_hbm, decode_hbm, out_ref, weight_ref, prefill_ref, decode_ref, sems
):
    copies = fetch(
        (weight_hbm, prefill_hbm, decode_hbm), (weight_ref, prefill_ref, decode_ref), sems
    )
    half = out_ref.shape[0] // 2
    copies[0].wait()
    weight = weight_ref[...]
    for part, ref in enumerate((prefill_ref, decode_ref)):
        copies[part + 1].wait()
        rows = lax.dot_general(
            ref[...], weight, (((1,), (1,)), ((), ())), preferred_element_type=jnp.float32
        )
        out_ref[part * half : (part + 1) * half] = rows.reshape(half, ref.shape[0] // half, -1)


def total_kernel(parts_ref, out_ref):
    total = jnp.sum(parts_ref[...], axis=0)
    out_ref[...] = jnp.broadcast_to(total[None], out_ref.shape)


def step_sizes(proj, weight_ref, bias_ref):
    rank = weight_ref.shape[0]
    low = proj[:, :rank].astype(jnp.bfloat16)
    return softplus(
        jnp.dot(low, weight_ref[...], preferred_element_type=jnp.float32) + bias_ref[...]
    )


def advance(hidden, rates_ref, size_row, forcing_row, inject, readout):
    mixed = []
    for tile, cols in enumerate(tiles_of(size_row.shape[1])):
        damping = jnp.exp2(size_row[:, cols] * rates_ref[:, cols])
        hidden[tile] = damping * hidden[tile] + forcing_row[:, cols] * inject
        if readout is not None:
            mixed.append(jnp.sum(readout * hidden[tile], axis=0, keepdims=True))
    return jnp.concatenate(mixed, axis=1) if mixed else None


def prepare_scan(lengths_ref, proj, x_ref, weight_ref, bias_ref, alog_ref, size_ref, force_ref, vec_ref, rates_ref):
    tokens, channels = x_ref.shape
    size = step_sizes(proj, weight_ref, bias_ref)
    force_ref[...] = size * x_ref[...].astype(jnp.float32)
    position = lax.broadcasted_iota(jnp.int32, (tokens, LANES), 0)
    first = position == 0
    begin = jnp.int32(0)
    ends = []
    for k in range(lengths_ref.shape[1]):
        first = first | (position == begin)
        begin = begin + lengths_ref[0, k]
        ends.append(begin - 1)
    reset = jnp.where(first, jnp.float32(FAR), jnp.float32(0.0))
    for cols in tiles_of(channels):
        size_ref[:, cols] = size[:, cols] + reset
    vec_ref[...] = jnp.transpose(proj[:, weight_ref.shape[0] :])
    rates_ref[...] = -LOG2E * jnp.exp(alog_ref[...])
    return ends


def scan(size_ref, force_ref, vec_ref, rates_ref, mixed_ref, hist_ref):
    tokens, channels = size_ref.shape
    width = rates_ref.shape[0]
    tiles = tiles_of(channels)

    def block(b, hidden):
        base = pl.multiple_of(b * 8, 8)
        vectors = pltpu.roll(vec_ref[...], tokens - base, axis=1)
        sizes = size_ref[pl.ds(base, 8), :]
        forces = force_ref[pl.ds(base, 8), :]
        hidden = list(hidden)
        rows = []
        for i in range(8):
            inject = jnp.broadcast_to(vectors[:width, i : i + 1], (width, LANES))
            readout = None
            if mixed_ref is not None:
                readout = jnp.broadcast_to(vectors[width:, i : i + 1], (width, LANES))
            rows.append(
                advance(hidden, rates_ref, sizes[i : i + 1], forces[i : i + 1], inject, readout)
            )
            if hist_ref is not None:
                for tile, cols in enumerate(tiles):
                    hist_ref[base + i, :, cols] = hidden[tile]
        if mixed_ref is not None:
            mixed_ref[pl.ds(base, 8), :] = jnp.concatenate(rows, axis=0)
        return tuple(hidden)

    zero = jnp.zeros((width, LANES), jnp.float32)
    lax.fori_loop(0, tokens // 8, block, (zero,) * len(tiles))


def states_kernel(
    lengths_ref, routes_ref, proj_ref, x_ref, weight_ref, bias_ref, alog_ref,
    send_ref, size_ref, force_ref, vec_ref, rates_ref, hist_ref, sems,
):
    requests = lengths_ref.shape[1]
    group = lax.axis_index("group")
    proj = proj_ref[...].reshape(x_ref.shape[0], -1)
    ends = prepare_scan(
        lengths_ref, proj, x_ref, weight_ref, bias_ref, alog_ref, size_ref, force_ref, vec_ref,
        rates_ref,
    )
    scan(size_ref, force_ref, vec_ref, rates_ref, None, hist_ref)
    dests = [routes_ref[group * requests + k, 0] for k in range(requests)]
    copies = []
    for k in range(requests):
        lane = jnp.int32(0)
        for j in range(k):
            lane = lane + (dests[j] == dests[k]).astype(jnp.int32)
        copies.append(
            pltpu.make_async_copy(hist_ref.at[ends[k]], send_ref.at[dests[k], lane], sems.at[k])
        )
        copies[-1].start()
    for copy in copies:
        copy.wait()


def rest_kernel(
    lengths_ref, routes_ref, proj_ref,
    state_hbm, decode_x_hbm, decode_gate_hbm, weight_hbm, alog_hbm, bias_hbm, skip_hbm,
    prefill_x_hbm, prefill_gate_hbm,
    out_ref, mixed_ref, unit_ref, source_ref,
    state_ref, decode_x_ref, decode_gate_ref, weight_ref, alog_ref, bias_ref, skip_ref,
    prefill_x_ref, prefill_gate_ref,
    size_ref, force_ref, act_ref, sum_ref, vec_ref, rates_ref, sems, *, groups,
):
    copies = fetch(
        (
            weight_hbm, alog_hbm, bias_hbm, skip_hbm, decode_x_hbm, decode_gate_hbm, state_hbm,
            prefill_x_hbm, prefill_gate_hbm,
        ),
        (
            weight_ref, alog_ref, bias_ref, skip_ref, decode_x_ref, decode_gate_ref, state_ref,
            prefill_x_ref, prefill_gate_ref,
        ),
        sems,
    )
    total, channels = decode_x_ref.shape
    rows, width = state_ref.shape[:2]
    steps = total // rows
    reach = unit_ref.shape[0]
    half = proj_ref.shape[0] // 2
    tiles = tiles_of(channels)
    rank = weight_ref.shape[0]
    requests = lengths_ref.shape[1]
    me = lax.axis_index("group")
    for n in range(reach):
        source_ref[n] = -1
    slot = jnp.int32(0)
    for g in range(groups):
        lane = jnp.int32(0)
        for k in range(requests):
            ours = routes_ref[g * requests + k, 0] == me

            @pl.when(ours)
            def _(g=g, slot=slot, lane=lane):
                source_ref[slot] = g * CAP + lane

            slot = slot + ours.astype(jnp.int32)
            lane = lane + ours.astype(jnp.int32)

    for copy in copies[:5]:
        copy.wait()
    proj = proj_ref[half:].reshape(total, -1)
    size = step_sizes(proj, weight_ref, bias_ref)
    values = decode_x_ref[...].astype(jnp.float32)
    size_ref[...] = size
    force_ref[...] = size * values
    vec_ref[...] = jnp.transpose(proj[:, rank:])
    rates_ref[...] = -LOG2E * jnp.exp(alog_ref[...])
    copies[5].wait()
    act_ref[...] = silu(decode_gate_ref[...].astype(jnp.float32))
    copies[6].wait()

    def block(b, carry, units):
        base = pl.multiple_of(b * 8, 8)
        at = [pl.multiple_of(s * rows + base, 8) for s in range(steps)]
        vectors = [pltpu.roll(vec_ref[...], total - at[s], axis=1) for s in range(steps)]
        sizes = [size_ref[pl.ds(at[s], 8), :] for s in range(steps)]
        forces = [force_ref[pl.ds(at[s], 8), :] for s in range(steps)]
        acts = [act_ref[pl.ds(at[s], 8), :] for s in range(steps)]
        results = [[] for _ in range(steps)]
        for i in range(8):
            hidden = [state_ref[base + i, :, cols] for cols in tiles]
            if units:
                taken = source_ref[base + i] >= 0
                hidden = [jnp.where(taken, 0.0, start) for start in hidden]
            summed = None
            for s in range(steps):
                inject = jnp.broadcast_to(vectors[s][:width, i : i + 1], (width, LANES))
                readout = jnp.broadcast_to(vectors[s][width:, i : i + 1], (width, LANES))
                row = sizes[s][i : i + 1]
                results[s].append(
                    advance(hidden, rates_ref, row, forces[s][i : i + 1], inject, readout)
                )
                if units:
                    summed = row if s == 0 else summed + row
                    for cols in tiles:
                        unit_ref[base + i, s, :, cols] = (
                            readout * acts[s][i : i + 1, cols]
                        ) * jnp.exp2(summed[:, cols] * rates_ref[:, cols])
        for s in range(steps):
            sum_ref[pl.ds(at[s], 8), :] = jnp.concatenate(results[s], axis=0)
        return carry

    lax.fori_loop(0, reach // 8, functools.partial(block, units=True), 0)
    lax.fori_loop(reach // 8, rows // 8, functools.partial(block, units=False), 0)
    mixed_ref[...] = (sum_ref[...] + skip_ref[...] * values) * act_ref[...]

    copies[7].wait()
    proj = proj_ref[:half].reshape(total, -1)
    prepare_scan(
        lengths_ref, proj, prefill_x_ref, weight_ref, bias_ref, alog_ref, size_ref, force_ref,
        vec_ref, rates_ref,
    )
    scan(size_ref, force_ref, vec_ref, rates_ref, sum_ref, None)
    copies[8].wait()
    mixed = sum_ref[...] + skip_ref[...] * prefill_x_ref[...].astype(jnp.float32)
    out_ref[...] = (mixed * silu(prefill_gate_ref[...].astype(jnp.float32))).astype(out_ref.dtype)


def combine_kernel(source_ref, mixed_ref, unit_ref, recv_ref, out_ref):
    reach, steps = unit_ref.shape[:2]
    rows = mixed_ref.shape[0] // steps
    added = [[] for _ in range(steps)]
    for n in range(reach):
        source = source_ref[n]
        state = jnp.where(source >= 0, recv_ref[jnp.maximum(source, 0)], 0.0)
        for s in range(steps):
            added[s].append(jnp.sum(unit_ref[n, s] * state, axis=0, keepdims=True))
    for s in range(steps):
        first, last = s * rows, (s + 1) * rows
        out_ref[first : first + reach, :] = (
            mixed_ref[first : first + reach, :] + jnp.concatenate(added[s], axis=0)
        ).astype(out_ref.dtype)
        out_ref[first + reach : last, :] = mixed_ref[first + reach : last, :].astype(out_ref.dtype)


def local(
    prefill_x, prefill_gate, lengths, routes, decode_x, decode_gate, cached_state, xproj_weight,
    dt_weight, dt_bias, a_log, skip_gain, *, ranks, groups,
):
    tokens, channels = prefill_x.shape
    steps, rows, _ = decode_x.shape
    width = a_log.shape[0]
    requests = lengths.shape[1]
    columns = xproj_weight.shape[1]
    total = steps * rows
    reach = groups * CAP
    decode_flat = decode_x.reshape(total, channels)
    gate_flat = decode_gate.reshape(total, channels)
    bias = dt_bias.reshape(1, channels)
    skip = skip_gain.reshape(1, channels)
    per = (tokens + total) // ranks
    chunked = struct((ranks, per, columns))

    partial = call(
        project_kernel, "project", chunked, [ANY] * 3,
        scratch=[
            bf16(columns, channels), bf16(tokens, channels), bf16(total, channels),
            pltpu.SemaphoreType.DMA((3,)),
        ],
    )(*stay(xproj_weight.T, prefill_x, decode_flat))
    parts = lax.all_to_all(partial, "tp", 0, 0)
    copies = call(total_kernel, "total", chunked, [VMEM])(parts)
    proj = lax.all_to_all(copies, "tp", 0, 0)

    scan_scratch = [
        f32(tokens, channels), f32(tokens, channels), f32(2 * width, tokens), f32(width, channels)
    ]
    send = call(
        states_kernel, "states", struct((groups, CAP, width, channels)),
        [SMEM, SMEM, pl.BlockSpec((ranks // 2, per, columns), lambda i: (0, 0, 0))] + [VMEM] * 4,
        out_specs=ANY,
        scratch=scan_scratch
        + [f32(tokens, width, channels), pltpu.SemaphoreType.DMA((requests,))],
    )(lengths, routes, proj, prefill_x, dt_weight, bias, a_log)
    recv = lax.all_to_all(send, "group", 0, 0)
    prefill_out, mixed, unit, source = call(
        functools.partial(rest_kernel, groups=groups), "rest",
        (
            struct((tokens, channels), jnp.bfloat16), struct((total, channels)),
            struct((reach, steps, width, channels)), struct((reach,), jnp.int32),
        ),
        [SMEM, SMEM, VMEM] + [ANY] * 9,
        out_specs=(VMEM, VMEM, VMEM, SMEM),
        scratch=[
            f32(rows, width, channels), bf16(total, channels), bf16(total, channels),
            bf16(*dt_weight.shape), f32(width, channels), f32(1, channels), f32(1, channels),
            bf16(tokens, channels), bf16(tokens, channels),
            f32(total, channels), f32(total, channels), f32(total, channels),
            f32(total, channels), f32(2 * width, total), f32(width, channels),
            pltpu.SemaphoreType.DMA((9,)),
        ],
        flops=8 * 10**9,
    )(
        lengths, routes, proj,
        *stay(
            cached_state, decode_flat, gate_flat, dt_weight, a_log, bias, skip, prefill_x,
            prefill_gate,
        ),
    )
    decode_out = call(
        combine_kernel, "combine", struct((total, channels), jnp.bfloat16), [SMEM] + [VMEM] * 3
    )(source, mixed, unit, recv.reshape(reach, width, channels))
    return prefill_out, decode_out.reshape(steps, rows, channels)


def solution(mesh):
    placed = (
        P("group", "tp"), P("group", "tp"), P("group", None), P(), P(None, "group", "tp"),
        P(None, "group", "tp"), P("group", None, "tp"), P("tp", None), P(None, "tp"), P("tp"),
        P(None, "tp"), P("tp"),
    )
    body = functools.partial(local, ranks=mesh.shape["tp"], groups=mesh.shape["group"])
    return jax.shard_map(
        body, mesh=mesh, in_specs=placed, out_specs=(P("group", "tp"), P(None, "group", "tp")),
        check_vma=False,
    )
```

time: 77.7 us -> 73.7 us (0.949)
  blocking collectives: 48.3 us -> 21.6 us
  starting transfers between devices: 4.04 us -> 14.5 us
  Pallas kernels: 11.3 us -> 18.9 us
  waiting for transfers between devices: 11.5 us -> 16.6 us
    all_to_all x1 -> x0, blocking collectives: 26.9 us -> none  [local(): recv = lax.all_to_all(send, 'group', 0, 0)]
    all_to_all x0 -> x1, starting transfers between devices: none -> 10.6 us  [local(): recv = lax.all_to_all(send, 'group', 0, 0)]
    pallas_call x4 -> x5, Pallas kernels: 11.3 us -> 18.9 us  [the longest x1 9.68 us: local(): call(functools.partial(rest_kernel, groups=groups), 'rest', (struct((toke...]
    all_to_all x0 -> x1, waiting for transfers between devices: none -> 5.15 us  [local(): recv = lax.all_to_all(send, 'group', 0, 0)]
  transfers between devices with their start and end apart: 1 -> 2, of which waited for: 1 -> 2; matrix products, arithmetic and copies ran while one was open for 0% -> 0% of each run, Pallas kernels for 0% -> 13%
where the time goes in v2:
time: 73.7 us; the launch traced here: 73.3 us
  blocking collectives  21.6 us (29%)
  Pallas kernels  18.9 us (26%)
  waiting for transfers between devices  16.6 us (23%)
  starting transfers between devices  14.5 us (20%)
  local copies, waits for them, and re-layouts  0.9 us (1%)
  between operations  0.74 us (1%)
    all_to_all x1, blocking collectives, local(): parts = lax.all_to_all(partial, 'tp', 0, 0)  21.6 us
    all_to_all x1, waiting for transfers between devices, local(): proj = lax.all_to_all(copies, 'tp', 0, 0)  11.5 us
    all_to_all x1, starting transfers between devices, local(): recv = lax.all_to_all(send, 'group', 0, 0)  10.6 us
    pallas_call x1, Pallas kernels, local(): call(functools.partial(rest_kernel, groups=groups), 'rest', (struct((toke...  9.68 us
    all_to_all x1, waiting for transfers between devices, local(): recv = lax.all_to_all(send, 'group', 0, 0)  5.15 us
    pallas_call x1, Pallas kernels, local(): call(states_kernel, 'states', struct((groups, CAP, width, channels)), [SM...  4.91 us
    all_to_all x1, starting transfers between devices, local(): proj = lax.all_to_all(copies, 'tp', 0, 0)  3.9 us
    pallas_call x1, Pallas kernels, local(): call(project_kernel, 'project', chunked, [ANY] * 3, scratch=[bf16(columns...  1.86 us
  transfers between devices with their start and end apart: 2, of which 2 were waited for; matrix products, arithmetic and copies ran while one was open for 0% of the time, Pallas kernels for 13%

profile of v2, /device:TPU:1, one launch (start us, length us, event | category | flops | bytes accessed | tf_op | source)
XLA Modules:
  0.0 73.3 jit_solution(2544860709031926028)
XLA Ops:
  0.6 1.9 %project.1 = f32[32,8,544]{2,1,0:T(8,128)S(1)} custom-call(bf16[544,512]{1,0:T(8,128)(2,1)} %bitcast.10, bf16[128,512]{1,0:T(8,128)(2,1)} %x_ref.1, bf16[128,512]{1,0:T(8,128)(2,1)} %bitcast.11), custom_call_target="tpu_custom_call" | custom-call | bytes 1048576 | tf_op jit(solution)/shard_map/project/pallas_call | solution.py:327
  2.5 0.0 copy-start.7
  2.5 0.0 copy-start
  2.5 0.0 copy-start.1
  2.5 0.0 copy-start.4
  2.5 0.0 copy-start.5
  2.6 0.0 copy-start.6
  2.6 21.6 %all_to_all.15.parts_ref = f32[32,8,544]{2,1,0:T(8,128)S(1)} all-to-all(f32[32,8,544]{2,1,0:T(8,128)S(1)} %project.1), channel_id=1, replica_groups=mesh['group'=8,'tp'=32] {'tp'}, dimensions={0} | all-to-all | bytes 1114112 | tf_op jit(solution)/shard_map/all_to_all | solution.py:334
  24.1 0.9 %total.1 = f32[32,8,544]{2,1,0:T(8,128)} custom-call(f32[32,8,544]{2,1,0:T(8,128)S(1)} %all_to_all.15.parts_ref), custom_call_target="tpu_custom_call" | custom-call | bytes 1048576 | tf_op jit(solution)/shard_map/total/pallas_call | solution.py:335
  25.1 3.9 %all-to-all-start.1 = ((f32[32,8,544]{2,1,0:T(8,128)}), f32[32,8,544]{2,1,0:T(8,128)S(1)}, u32[]{:S(2)}, u32[]{:S(2)}) async-start(f32[32,8,544]{2,1,0:T(8,128)} %total.1), calls=%async_computation.1 | async-start | bytes 1310720 | tf_op jit(solution)/shard_map/all_to_all | solution.py:336
  29.0 0.0 copy-done.7
  29.0 0.1 copy.14.routes_ref
  29.1 0.0 copy-start.2
  29.1 11.5 %all-to-all-done.1.proj_ref = f32[32,8,544]{2,1,0:T(8,128)S(1)} async-done(((f32[32,8,544]{2,1,0:T(8,128)}), f32[32,8,544]{2,1,0:T(8,128)S(1)}, u32[]{:S(2)}, u32[]{:S(2)}) %all-to-all-start.1) | async-done | bytes 557088 | tf_op jit(solution)/shard_map/all_to_all | solution.py:336
  40.6 0.0 copy-done
  40.6 0.0 copy-done.1
  40.6 0.0 copy-done.4
  40.6 0.0 copy-done.5
  40.6 0.0 copy-done.6
  40.6 4.9 %states.1 = f32[8,2,16,512]{3,2,1,0:T(8,128)} custom-call(s32[1,8]{1,0:T(1,128)S(1)} %copy-done.6, s32[64,1]{1,0:T(8,128)S(1)} %copy.14.routes_ref, f32[32,8,544]{2,1,0:T(8,128)S(1)} %all-to-all-done.1.proj_ref, bf16[128,512]{1,0:T(8,128)(2,1)S(1)} %copy-done.1, bf16[512,512]{1,0:T(8,128)(2,1)S(1)} %copy-done, f32[1,512]{1,0:T(1,128)S(1)} %bitcast.9, ...), custom_call_target="tpu_custom_call" | custom-call | bytes 1048576 | tf_op jit(solution)/shard_map/states/pallas_call | solution.py:341
  45.5 10.6 %all-to-all-start.2 = ((f32[8,2,16,512]{3,2,1,0:T(8,128)}), f32[8,2,16,512]{3,2,1,0:T(8,128)S(1)}, u32[]{:S(2)}, u32[]{:S(2)}) async-start(f32[8,2,16,512]{3,2,1,0:T(8,128)} %states.1), calls=%async_computation.2 | async-start | bytes 1048576 | tf_op jit(solution)/shard_map/all_to_all | solution.py:348
  56.1 0.0 copy-done.2
  56.1 0.0 copy-start.3
  56.1 0.8 %copy-done.3 = s32[64,1]{1,0:T(8,128)S(1)} copy-done((s32[64,1]{1,0:T(8,128)S(1)}, s32[64,1]{1,0:T(8,128)}, u32[]{:S(2)}) %copy-start.3) | copy-done | bytes 280
  56.9 9.7 %rest.1 = (bf16[128,512]{1,0:T(8,128)(2,1)}, f32[128,512]{1,0:T(8,128)S(1)}, f32[16,4,16,512]{3,2,1,0:T(8,128)S(1)}, s32[16]{0:T(128)S(1)}) custom-call(s32[1,8]{1,0:T(1,128)S(1)} %copy-done.6, s32[64,1]{1,0:T(8,128)S(1)} %copy-done.3, f32[32,8,544]{2,1,0:T(8,128)S(1)} %all-to-all-done.1.proj_ref, f32[32,16,512]{2,1,0:T(8,128)} %state_hbm.1, ...), custom_call_target="tpu_custom_call" | custom-call | flops 8000000000 | bytes 1048576 | tf_op jit(solution)/shard_map/rest/pallas_call | solution.py:349
  66.6 5.1 %all-to-all-done.2 = f32[8,2,16,512]{3,2,1,0:T(8,128)S(1)} async-done(((f32[8,2,16,512]{3,2,1,0:T(8,128)}), f32[8,2,16,512]{3,2,1,0:T(8,128)S(1)}, u32[]{:S(2)}, u32[]{:S(2)}) %all-to-all-start.2) | async-done | bytes 524320 | tf_op jit(solution)/shard_map/all_to_all | solution.py:348
  71.7 1.6 %combine.1 = bf16[128,512]{1,0:T(8,128)(2,1)} custom-call(s32[16]{0:T(128)S(1)} %get-tuple-element.7.source_ref, f32[128,512]{1,0:T(8,128)S(1)} %get-tuple-element.8.mixed_ref, f32[16,4,16,512]{3,2,1,0:T(8,128)S(1)} %get-tuple-element.9.unit_ref, f32[16,16,512]{2,1,0:T(8,128)S(1)} %bitcast.7), custom_call_target="tpu_custom_call" | custom-call | bytes 1048576 | tf_op jit(solution)/shard_map/combine/pallas_call | solution.py:373
Async XLA Ops:
  2.5 26.5 %copy-start.7 = (s32[64,1]{0,1:T(1,128)S(1)}, s32[64,1]{0,1:T(1,128)}, u32[]{:S(2)}) copy-start(s32[64,1]{0,1:T(1,128)} %param.15) | copy-start | bytes 772
  2.5 38.1 %copy-start = (bf16[512,512]{1,0:T(8,128)(2,1)S(1)}, bf16[512,512]{1,0:T(8,128)(2,1)}, u32[]{:S(2)}) copy-start(bf16[512,512]{1,0:T(8,128)(2,1)} %weight_ref.1) | copy-start | bytes 1572868
  2.5 38.1 %copy-start.1 = (bf16[128,512]{1,0:T(8,128)(2,1)S(1)}, bf16[128,512]{1,0:T(8,128)(2,1)}, u32[]{:S(2)}) copy-start(bf16[128,512]{1,0:T(8,128)(2,1)} %x_ref.1) | copy-start | bytes 393220
  2.5 38.0 %copy-start.4 = (f32[16,512]{1,0:T(8,128)S(1)}, f32[16,512]{1,0:T(8,128)}, u32[]{:S(2)}) copy-start(f32[16,512]{1,0:T(8,128)} %alog_ref.1) | copy-start | bytes 98308
  2.5 38.0 %copy-start.5 = (f32[512]{0:T(512)S(1)}, f32[512]{0:T(512)}, u32[]{:S(2)}) copy-start(f32[512]{0:T(512)} %param.21) | copy-start | bytes 6148
  2.6 38.0 %copy-start.6 = (s32[1,8]{1,0:T(1,128)S(1)}, s32[1,8]{1,0:T(1,128)}, u32[]{:S(2)}) copy-start(s32[1,8]{1,0:T(1,128)} %lengths_ref.3) | copy-start | bytes 100
  25.1 15.5 %all-to-all-start.1 = ((f32[32,8,544]{2,1,0:T(8,128)}), f32[32,8,544]{2,1,0:T(8,128)S(1)}, u32[]{:S(2)}, u32[]{:S(2)}) async-start(f32[32,8,544]{2,1,0:T(8,128)} %total.1), calls=%async_computation.1 | async-start | bytes 1310720 | tf_op jit(solution)/shard_map/all_to_all | solution.py:336
  29.1 27.0 %copy-start.2 = (s32[64,1]{1,0:T(8,128)}, s32[64,1]{1,0:T(8,128)S(1)}, u32[]{:S(2)}) copy-start(s32[64,1]{1,0:T(8,128)S(1)} %copy.14.routes_ref) | copy-start | bytes 772
  45.5 26.2 %all-to-all-start.2 = ((f32[8,2,16,512]{3,2,1,0:T(8,128)}), f32[8,2,16,512]{3,2,1,0:T(8,128)S(1)}, u32[]{:S(2)}, u32[]{:S(2)}) async-start(f32[8,2,16,512]{3,2,1,0:T(8,128)} %states.1), calls=%async_computation.2 | async-start | bytes 1048576 | tf_op jit(solution)/shard_map/all_to_all | solution.py:348
  56.1 0.8 %copy-start.3 = (s32[64,1]{1,0:T(8,128)S(1)}, s32[64,1]{1,0:T(8,128)}, u32[]{:S(2)}) copy-start(s32[64,1]{1,0:T(8,128)} %copy-done.2) | copy-start | bytes 772

commit v3 on v2

--- a/solution.py
+++ b/solution.py
@@ -98,14 +98,29 @@
     )
 
 
-def advance(hidden, rates_ref, size_row, forcing_row, inject, readout):
-    mixed = []
+def fold(terms):
+    return sum(terms[i : i + 8] for i in range(8, terms.shape[0], 8)) + terms[:8]
+
+
+def gather_sums(part_ref, first, stride):
+    return jnp.concatenate(
+        [
+            sum(
+                (part_ref[tile, pl.ds(first + j, 8, stride=stride), :] for j in range(1, 8)),
+                part_ref[tile, pl.ds(first, 8, stride=stride), :],
+            )
+            for tile in range(part_ref.shape[0])
+        ],
+        axis=1,
+    )
+
+
+def advance(hidden, rates_ref, size_row, forcing_row, inject, readout, part_ref, at):
     for tile, cols in enumerate(tiles_of(size_row.shape[1])):
         damping = jnp.exp2(size_row[:, cols] * rates_ref[:, cols])
         hidden[tile] = damping * hidden[tile] + forcing_row[:, cols] * inject
         if readout is not None:
-            mixed.append(jnp.sum(readout * hidden[tile], axis=0, keepdims=True))
-    return jnp.concatenate(mixed, axis=1) if mixed else None
+            part_ref[tile, at : at + 8, :] = fold(readout * hidden[tile])
 
 
 def prepare_scan(lengths_ref, proj, x_ref, weight_ref, bias_ref, alog_ref, size_ref, force_ref, vec_ref, rates_ref):
@@ -128,7 +143,7 @@
     return ends
 
 
-def scan(size_ref, force_ref, vec_ref, rates_ref, mixed_ref, hist_ref):
+def scan(size_ref, force_ref, vec_ref, rates_ref, mixed_ref, part_ref, hist_ref):
     tokens, channels = size_ref.shape
     width = rates_ref.shape[0]
     tiles = tiles_of(channels)
@@ -139,24 +154,24 @@
         sizes = size_ref[pl.ds(base, 8), :]
         forces = force_ref[pl.ds(base, 8), :]
         hidden = list(hidden)
-        rows = []
         for i in range(8):
             inject = jnp.broadcast_to(vectors[:width, i : i + 1], (width, LANES))
             readout = None
             if mixed_ref is not None:
                 readout = jnp.broadcast_to(vectors[width:, i : i + 1], (width, LANES))
-            rows.append(
-                advance(hidden, rates_ref, sizes[i : i + 1], forces[i : i + 1], inject, readout)
+            advance(
+                hidden, rates_ref, sizes[i : i + 1], forces[i : i + 1], inject, readout,
+                part_ref, i * 8,
             )
             if hist_ref is not None:
                 for tile, cols in enumerate(tiles):
                     hist_ref[base + i, :, cols] = hidden[tile]
         if mixed_ref is not None:
-            mixed_ref[pl.ds(base, 8), :] = jnp.concatenate(rows, axis=0)
+            mixed_ref[pl.ds(base, 8), :] = gather_sums(part_ref, 0, 8)
         return tuple(hidden)
 
     zero = jnp.zeros((width, LANES), jnp.float32)
-    lax.fori_loop(0, tokens // 8, block, (zero,) * len(tiles))
+    lax.fori_loop(0, tokens // 8, block, (zero,) * len(tiles), unroll=16)
 
 
 def states_kernel(
@@ -170,8 +185,8 @@
         lengths_ref, proj, x_ref, weight_ref, bias_ref, alog_ref, size_ref, force_ref, vec_ref,
         rates_ref,
     )
-    scan(size_ref, force_ref, vec_ref, rates_ref, None, hist_ref)
-    dests = [routes_ref[group * requests + k, 0] for k in range(requests)]
+    scan(size_ref, force_ref, vec_ref, rates_ref, None, None, hist_ref)
+    dests = [routes_ref[0, group * requests + k] for k in range(requests)]
     copies = []
     for k in range(requests):
         lane = jnp.int32(0)
@@ -192,7 +207,7 @@
     out_ref, mixed_ref, unit_ref, source_ref,
     state_ref, decode_x_ref, decode_gate_ref, weight_ref, alog_ref, bias_ref, skip_ref,
     prefill_x_ref, prefill_gate_ref,
-    size_ref, force_ref, act_ref, sum_ref, vec_ref, rates_ref, sems, *, groups,
+    size_ref, force_ref, act_ref, sum_ref, part_ref, vec_ref, rates_ref, sems, *, groups,
 ):
     copies = fetch(
         (
@@ -220,7 +235,7 @@
     for g in range(groups):
         lane = jnp.int32(0)
         for k in range(requests):
-            ours = routes_ref[g * requests + k, 0] == me
+            ours = routes_ref[0, g * requests + k] == me
 
             @pl.when(ours)
             def _(g=g, slot=slot, lane=lane):
@@ -249,7 +264,6 @@
         sizes = [size_ref[pl.ds(at[s], 8), :] for s in range(steps)]
         forces = [force_ref[pl.ds(at[s], 8), :] for s in range(steps)]
         acts = [act_ref[pl.ds(at[s], 8), :] for s in range(steps)]
-        results = [[] for _ in range(steps)]
         for i in range(8):
             hidden = [state_ref[base + i, :, cols] for cols in tiles]
             if units:
@@ -260,8 +274,9 @@
                 inject = jnp.broadcast_to(vectors[s][:width, i : i + 1], (width, LANES))
                 readout = jnp.broadcast_to(vectors[s][width:, i : i + 1], (width, LANES))
                 row = sizes[s][i : i + 1]
-                results[s].append(
-                    advance(hidden, rates_ref, row, forces[s][i : i + 1], inject, readout)
+                advance(
+                    hidden, rates_ref, row, forces[s][i : i + 1], inject, readout, part_ref,
+                    (s * 8 + i) * 8,
                 )
                 if units:
                     summed = row if s == 0 else summed + row
@@ -270,7 +285,7 @@
                             readout * acts[s][i : i + 1, cols]
                         ) * jnp.exp2(summed[:, cols] * rates_ref[:, cols])
         for s in range(steps):
-            sum_ref[pl.ds(at[s], 8), :] = jnp.concatenate(results[s], axis=0)
+            sum_ref[pl.ds(at[s], 8), :] = gather_sums(part_ref, s * 64, 8)
         return carry
 
     lax.fori_loop(0, reach // 8, functools.partial(block, units=True), 0)
@@ -283,7 +298,7 @@
         lengths_ref, proj, prefill_x_ref, weight_ref, bias_ref, alog_ref, size_ref, force_ref,
         vec_ref, rates_ref,
     )
-    scan(size_ref, force_ref, vec_ref, rates_ref, sum_ref, None)
+    scan(size_ref, force_ref, vec_ref, rates_ref, sum_ref, part_ref, None)
     copies[8].wait()
     mixed = sum_ref[...] + skip_ref[...] * prefill_x_ref[...].astype(jnp.float32)
     out_ref[...] = (mixed * silu(prefill_gate_ref[...].astype(jnp.float32))).astype(out_ref.dtype)
@@ -322,6 +337,7 @@
     bias = dt_bias.reshape(1, channels)
     skip = skip_gain.reshape(1, channels)
     per = (tokens + total) // ranks
+    routes = routes.T
     chunked = struct((ranks, per, columns))
 
     partial = call(
@@ -359,8 +375,8 @@
             bf16(*dt_weight.shape), f32(width, channels), f32(1, channels), f32(1, channels),
             bf16(tokens, channels), bf16(tokens, channels),
             f32(total, channels), f32(total, channels), f32(total, channels),
-            f32(total, channels), f32(2 * width, total), f32(width, channels),
-            pltpu.SemaphoreType.DMA((9,)),
+            f32(total, channels), f32(channels // LANES, steps * 64, LANES), f32(2 * width, total),
+            f32(width, channels), pltpu.SemaphoreType.DMA((9,)),
         ],
         flops=8 * 10**9,
     )(

time: 73.7 us -> 69.8 us (0.947)
  blocking collectives: 21.6 us -> 36.3 us
  waiting for transfers between devices: 16.6 us -> 7.93 us
  Pallas kernels: 18.9 us -> 14.1 us
  starting transfers between devices: 14.5 us -> 10.4 us
  local copies, waits for them, and re-layouts: 0.9 us -> 0.04 us
    all_to_all x0 -> x1, blocking collectives: none -> 14.8 us  [local(): proj = lax.all_to_all(copies, 'tp', 0, 0)]
    all_to_all x1 -> x0, waiting for transfers between devices: 11.5 us -> none  [local(): proj = lax.all_to_all(copies, 'tp', 0, 0)]
    all_to_all x1 -> x0, starting transfers between devices: 3.9 us -> none  [local(): proj = lax.all_to_all(copies, 'tp', 0, 0)]
    all_to_all x1, waiting for transfers between devices: 5.15 us -> 7.93 us  [local(): recv = lax.all_to_all(send, 'group', 0, 0)]
    pallas_call x1, Pallas kernels: 9.68 us -> 7.66 us  [local(): call(functools.partial(rest_kernel, groups=groups), 'rest', (struct((toke...]
    pallas_call x1, Pallas kernels: 4.91 us -> 2.98 us  [local(): call(states_kernel, 'states', struct((groups, CAP, width, channels)), [SM...]
    unnamed x17 -> x12, local copies, waits for them, and re-layouts: 0.9 us -> 0.04 us
    pallas_call x1, Pallas kernels: 0.92 us -> 0.08 us  [local(): copies = call(total_kernel, 'total', chunked, [VMEM])(parts)]
  transfers between devices with their start and end apart: 2 -> 1, of which waited for: 2 -> 1; matrix products, arithmetic and copies ran while one was open for 0% -> 0% of each run, Pallas kernels for 13% -> 11%
where the time goes in v3:
time: 69.8 us; the launch traced here: 69.5 us
  blocking collectives  36.3 us (52%)
  Pallas kernels  14.1 us (20%)
  starting transfers between devices  10.4 us (15%)
  waiting for transfers between devices  7.93 us (11%)
  between operations  0.73 us (1%)
    all_to_all x1, blocking collectives, local(): parts = lax.all_to_all(partial, 'tp', 0, 0)  21.6 us
    all_to_all x1, blocking collectives, local(): proj = lax.all_to_all(copies, 'tp', 0, 0)  14.8 us
    all_to_all x1, starting transfers between devices, local(): recv = lax.all_to_all(send, 'group', 0, 0)  10.4 us
    all_to_all x1, waiting for transfers between devices, local(): recv = lax.all_to_all(send, 'group', 0, 0)  7.93 us
    pallas_call x1, Pallas kernels, local(): call(functools.partial(rest_kernel, groups=groups), 'rest', (struct((toke...  7.66 us
    pallas_call x1, Pallas kernels, local(): call(states_kernel, 'states', struct((groups, CAP, width, channels)), [SM...  2.98 us
    pallas_call x1, Pallas kernels, local(): call(project_kernel, 'project', chunked, [ANY] * 3, scratch=[bf16(columns...  1.86 us
    pallas_call x1, Pallas kernels, local(): call(combine_kernel, 'combine', struct((total, channels), jnp.bfloat16),...  1.55 us
  transfers between devices with their start and end apart: 1, of which 1 were waited for; matrix products, arithmetic and copies ran while one was open for 0% of the time, Pallas kernels for 11%

profile of v3, /device:TPU:1, one launch (start us, length us, event | category | flops | bytes accessed | tf_op | source)
XLA Modules:
  0.0 69.5 jit_solution(897071782163805636)
XLA Ops:
  0.6 1.9 %project.1 = f32[32,8,544]{2,1,0:T(8,128)S(1)} custom-call(bf16[544,512]{1,0:T(8,128)(2,1)} %bitcast.13, bf16[128,512]{1,0:T(8,128)(2,1)} %x_ref.1, bf16[128,512]{1,0:T(8,128)(2,1)} %bitcast.14), custom_call_target="tpu_custom_call" | custom-call | bytes 1048576 | tf_op jit(solution)/shard_map/project/pallas_call | solution.py:343
  2.5 0.0 copy-start
  2.5 0.0 copy-start.1
  2.5 0.0 copy-start.2
  2.5 0.0 copy-start.3
  2.5 0.0 copy-start.4
  2.6 0.0 copy-start.5
  2.6 21.6 %all_to_all.15.parts_ref = f32[32,8,544]{2,1,0:T(8,128)S(1)} all-to-all(f32[32,8,544]{2,1,0:T(8,128)S(1)} %project.1), channel_id=1, replica_groups=mesh['group'=8,'tp'=32] {'tp'}, dimensions={0} | all-to-all | bytes 1114112 | tf_op jit(solution)/shard_map/all_to_all | solution.py:350
  24.1 0.1 total.1
  24.2 14.8 %all_to_all.16.proj_ref = f32[32,8,544]{2,1,0:T(8,128)S(1)} all-to-all(f32[32,8,544]{2,1,0:T(8,128)S(1)} %total.1), channel_id=1, replica_groups=mesh['group'=8,'tp'=32] {'tp'}, dimensions={0} | all-to-all | bytes 1114112 | tf_op jit(solution)/shard_map/all_to_all | solution.py:352
  39.0 0.0 copy-done
  39.0 0.0 copy-done.1
  39.0 0.0 copy-done.2
  39.0 0.0 copy-done.3
  39.0 0.0 copy-done.4
  39.0 0.0 copy-done.5
  39.0 3.0 %states.1 = f32[8,2,16,512]{3,2,1,0:T(8,128)} custom-call(s32[1,8]{1,0:T(1,128)S(1)} %copy-done.4, s32[1,64]{1,0:T(1,128)S(1)} %bitcast.11, f32[32,8,544]{2,1,0:T(8,128)S(1)} %all_to_all.16.proj_ref, bf16[128,512]{1,0:T(8,128)(2,1)S(1)} %copy-done, bf16[512,512]{1,0:T(8,128)(2,1)S(1)} %copy-done.1, f32[1,512]{1,0:T(1,128)S(1)} %bitcast.10, ...), custom_call_target="tpu_custom_call" | custom-call | bytes 1048576 | tf_op jit(solution)/shard_map/states/pallas_call | solution.py:357
  42.0 10.4 %all-to-all-start.2 = ((f32[8,2,16,512]{3,2,1,0:T(8,128)}), f32[8,2,16,512]{3,2,1,0:T(8,128)S(1)}, u32[]{:S(2)}, u32[]{:S(2)}) async-start(f32[8,2,16,512]{3,2,1,0:T(8,128)} %states.1), calls=%async_computation.2 | async-start | bytes 1048576 | tf_op jit(solution)/shard_map/all_to_all | solution.py:364
  52.4 7.7 %rest.1 = (bf16[128,512]{1,0:T(8,128)(2,1)}, f32[128,512]{1,0:T(8,128)S(1)}, f32[16,4,16,512]{3,2,1,0:T(8,128)S(1)}, s32[16]{0:T(128)S(1)}) custom-call(s32[1,8]{1,0:T(1,128)S(1)} %copy-done.4, s32[1,64]{1,0:T(1,128)S(1)} %bitcast.12, f32[32,8,544]{2,1,0:T(8,128)S(1)} %all_to_all.16.proj_ref, f32[32,16,512]{2,1,0:T(8,128)} %state_hbm.1, ...), custom_call_target="tpu_custom_call" | custom-call | flops 8000000000 | bytes 1048576 | tf_op jit(solution)/shard_map/rest/pallas_call | solution.py:365
  60.1 7.9 %all-to-all-done.2 = f32[8,2,16,512]{3,2,1,0:T(8,128)S(1)} async-done(((f32[8,2,16,512]{3,2,1,0:T(8,128)}), f32[8,2,16,512]{3,2,1,0:T(8,128)S(1)}, u32[]{:S(2)}, u32[]{:S(2)}) %all-to-all-start.2) | async-done | bytes 524320 | tf_op jit(solution)/shard_map/all_to_all | solution.py:364
  68.0 1.6 %combine.1 = bf16[128,512]{1,0:T(8,128)(2,1)} custom-call(s32[16]{0:T(128)S(1)} %get-tuple-element.7.source_ref, f32[128,512]{1,0:T(8,128)S(1)} %get-tuple-element.8.mixed_ref, f32[16,4,16,512]{3,2,1,0:T(8,128)S(1)} %get-tuple-element.9.unit_ref, f32[16,16,512]{2,1,0:T(8,128)S(1)} %bitcast.8), custom_call_target="tpu_custom_call" | custom-call | bytes 1048576 | tf_op jit(solution)/shard_map/combine/pallas_call | solution.py:389
Async XLA Ops:
  2.5 36.5 %copy-start = (bf16[128,512]{1,0:T(8,128)(2,1)S(1)}, bf16[128,512]{1,0:T(8,128)(2,1)}, u32[]{:S(2)}) copy-start(bf16[128,512]{1,0:T(8,128)(2,1)} %x_ref.1) | copy-start | bytes 393220
  2.5 36.5 %copy-start.1 = (bf16[512,512]{1,0:T(8,128)(2,1)S(1)}, bf16[512,512]{1,0:T(8,128)(2,1)}, u32[]{:S(2)}) copy-start(bf16[512,512]{1,0:T(8,128)(2,1)} %weight_ref.1) | copy-start | bytes 1572868
  2.5 36.5 %copy-start.2 = (f32[16,512]{1,0:T(8,128)S(1)}, f32[16,512]{1,0:T(8,128)}, u32[]{:S(2)}) copy-start(f32[16,512]{1,0:T(8,128)} %alog_ref.1) | copy-start | bytes 98308
  2.5 36.5 %copy-start.3 = (f32[512]{0:T(512)S(1)}, f32[512]{0:T(512)}, u32[]{:S(2)}) copy-start(f32[512]{0:T(512)} %param.21) | copy-start | bytes 6148
  2.5 36.5 %copy-start.4 = (s32[1,8]{1,0:T(1,128)S(1)}, s32[1,8]{1,0:T(1,128)}, u32[]{:S(2)}) copy-start(s32[1,8]{1,0:T(1,128)} %lengths_ref.3) | copy-start | bytes 100
  2.6 36.5 %copy-start.5 = (s32[64,1]{0,1:T(1,128)S(1)}, s32[64,1]{0,1:T(1,128)}, u32[]{:S(2)}) copy-start(s32[64,1]{0,1:T(1,128)} %param.15) | copy-start | bytes 772
  42.0 26.0 %all-to-all-start.2 = ((f32[8,2,16,512]{3,2,1,0:T(8,128)}), f32[8,2,16,512]{3,2,1,0:T(8,128)S(1)}, u32[]{:S(2)}, u32[]{:S(2)}) async-start(f32[8,2,16,512]{3,2,1,0:T(8,128)} %states.1), calls=%async_computation.2 | async-start | bytes 1048576 | tf_op jit(solution)/shard_map/all_to_all | solution.py:364

commit v4 on v3

--- a/solution.py
+++ b/solution.py
@@ -68,31 +68,65 @@
     return [slice(t, t + LANES) for t in range(0, channels, LANES)]
 
 
+def low_rows(rank, j, tile):
+    first = j * (8 * (rank // LANES) + 2) + 8 * tile
+    return slice(first, first + 8)
+
+
+def vector_rows(rank, count, which):
+    height = 8 * (rank // LANES) + 2
+    return pl.ds(height - 2 + which, count, stride=height)
+
+
+def low_part(proj_ref, rank, half, which):
+    tiles = range(rank // LANES)
+    return jnp.concatenate(
+        [
+            jnp.concatenate([proj_ref[low_rows(rank, j, tile), :] for tile in tiles], axis=1)
+            for j in range(half * which, half * (which + 1))
+        ],
+        axis=0,
+    )
+
+
 def project_kernel(
-    weight_hbm, prefill_hbm, decode_hbm, out_ref, weight_ref, prefill_ref, decode_ref, sems
+    weight_hbm, prefill_hbm, decode_hbm, out_ref, weight_ref, prefill_ref, decode_ref, sems,
+    *, rank,
 ):
     copies = fetch(
         (weight_hbm, prefill_hbm, decode_hbm), (weight_ref, prefill_ref, decode_ref), sems
     )
-    half = out_ref.shape[0] // 2
+    count = weight_ref.shape[0] - rank
+    half = count // 2
     copies[0].wait()
-    weight = weight_ref[...]
-    for part, ref in enumerate((prefill_ref, decode_ref)):
-        copies[part + 1].wait()
-        rows = lax.dot_general(
-            ref[...], weight, (((1,), (1,)), ((), ())), preferred_element_type=jnp.float32
+    for which, ref in enumerate((prefill_ref, decode_ref)):
+        copies[which + 1].wait()
+        values = ref[...]
+        low = lax.dot_general(
+            values, weight_ref[:rank], (((1,), (1,)), ((), ())), preferred_element_type=jnp.float32
         )
-        out_ref[part * half : (part + 1) * half] = rows.reshape(half, ref.shape[0] // half, -1)
-
-
-def total_kernel(parts_ref, out_ref):
-    total = jnp.sum(parts_ref[...], axis=0)
-    out_ref[...] = jnp.broadcast_to(total[None], out_ref.shape)
-
-
-def step_sizes(proj, weight_ref, bias_ref):
-    rank = weight_ref.shape[0]
-    low = proj[:, :rank].astype(jnp.bfloat16)
+        for j in range(half):
+            for tile, cols in enumerate(tiles_of(rank)):
+                out_ref[low_rows(rank, half * which + j, tile), :] = low[8 * j : 8 * j + 8, cols]
+        out_ref[vector_rows(rank, count, which), :] = lax.dot_general(
+            weight_ref[rank:], values, (((1,), (1,)), ((), ())), preferred_element_type=jnp.float32
+        )
+
+
+def total_kernel(parts_ref, out_ref, *, ranks):
+    height = parts_ref.shape[0] // ranks
+    group = 4
+    quad = parts_ref[...].reshape(ranks // group, group * height, LANES).sum(axis=0)
+    total = quad[:height]
+    for i in range(1, group):
+        total = total + quad[i * height : (i + 1) * height]
+    quad = jnp.concatenate([total] * group, axis=0)
+    for i in range(ranks // group):
+        out_ref[i * group * height : (i + 1) * group * height, :] = quad
+
+
+def step_sizes(low, weight_ref, bias_ref):
+    low = low.astype(jnp.bfloat16)
     return softplus(
         jnp.dot(low, weight_ref[...], preferred_element_type=jnp.float32) + bias_ref[...]
     )
@@ -123,9 +157,12 @@
             part_ref[tile, at : at + 8, :] = fold(readout * hidden[tile])
 
 
-def prepare_scan(lengths_ref, proj, x_ref, weight_ref, bias_ref, alog_ref, size_ref, force_ref, vec_ref, rates_ref):
+def prepare_scan(lengths_ref, proj_ref, x_ref, weight_ref, bias_ref, alog_ref, size_ref, force_ref, vec_ref, rates_ref):
     tokens, channels = x_ref.shape
-    size = step_sizes(proj, weight_ref, bias_ref)
+    rank = weight_ref.shape[0]
+    count = vec_ref.shape[0]
+    low = low_part(proj_ref, rank, count // 2, 0)
+    size = step_sizes(low, weight_ref, bias_ref)
     force_ref[...] = size * x_ref[...].astype(jnp.float32)
     position = lax.broadcasted_iota(jnp.int32, (tokens, LANES), 0)
     first = position == 0
@@ -138,7 +175,7 @@
     reset = jnp.where(first, jnp.float32(FAR), jnp.float32(0.0))
     for cols in tiles_of(channels):
         size_ref[:, cols] = size[:, cols] + reset
-    vec_ref[...] = jnp.transpose(proj[:, weight_ref.shape[0] :])
+    vec_ref[...] = proj_ref[vector_rows(rank, count, 0), :]
     rates_ref[...] = -LOG2E * jnp.exp(alog_ref[...])
     return ends
 
@@ -180,9 +217,8 @@
 ):
     requests = lengths_ref.shape[1]
     group = lax.axis_index("group")
-    proj = proj_ref[...].reshape(x_ref.shape[0], -1)
     ends = prepare_scan(
-        lengths_ref, proj, x_ref, weight_ref, bias_ref, alog_ref, size_ref, force_ref, vec_ref,
+        lengths_ref, proj_ref, x_ref, weight_ref, bias_ref, alog_ref, size_ref, force_ref, vec_ref,
         rates_ref,
     )
     scan(size_ref, force_ref, vec_ref, rates_ref, None, None, hist_ref)
@@ -224,9 +260,9 @@
     rows, width = state_ref.shape[:2]
     steps = total // rows
     reach = unit_ref.shape[0]
-    half = proj_ref.shape[0] // 2
     tiles = tiles_of(channels)
     rank = weight_ref.shape[0]
+    count = vec_ref.shape[0]
     requests = lengths_ref.shape[1]
     me = lax.axis_index("group")
     for n in range(reach):
@@ -246,12 +282,11 @@
 
     for copy in copies[:5]:
         copy.wait()
-    proj = proj_ref[half:].reshape(total, -1)
-    size = step_sizes(proj, weight_ref, bias_ref)
+    size = step_sizes(low_part(proj_ref, rank, count // 2, 1), weight_ref, bias_ref)
     values = decode_x_ref[...].astype(jnp.float32)
     size_ref[...] = size
     force_ref[...] = size * values
-    vec_ref[...] = jnp.transpose(proj[:, rank:])
+    vec_ref[...] = proj_ref[vector_rows(rank, count, 1), :]
     rates_ref[...] = -LOG2E * jnp.exp(alog_ref[...])
     copies[5].wait()
     act_ref[...] = silu(decode_gate_ref[...].astype(jnp.float32))
@@ -293,9 +328,8 @@
     mixed_ref[...] = (sum_ref[...] + skip_ref[...] * values) * act_ref[...]
 
     copies[7].wait()
-    proj = proj_ref[:half].reshape(total, -1)
     prepare_scan(
-        lengths_ref, proj, prefill_x_ref, weight_ref, bias_ref, alog_ref, size_ref, force_ref,
+        lengths_ref, proj_ref, prefill_x_ref, weight_ref, bias_ref, alog_ref, size_ref, force_ref,
         vec_ref, rates_ref,
     )
     scan(size_ref, force_ref, vec_ref, rates_ref, sum_ref, part_ref, None)
@@ -336,27 +370,33 @@
     gate_flat = decode_gate.reshape(total, channels)
     bias = dt_bias.reshape(1, channels)
     skip = skip_gain.reshape(1, channels)
-    per = (tokens + total) // ranks
+    rank = dt_weight.shape[0]
+    height = 8 * (rank // LANES) + 2
     routes = routes.T
-    chunked = struct((ranks, per, columns))
+    flat = struct((ranks * height, LANES))
+
+    def exchange(rows):
+        chunks = rows.reshape(ranks, height // 2, 2, LANES)
+        return lax.all_to_all(chunks, "tp", 0, 0).reshape(ranks * height, LANES)
 
     partial = call(
-        project_kernel, "project", chunked, [ANY] * 3,
+        functools.partial(project_kernel, rank=rank), "project", flat, [ANY] * 3,
         scratch=[
             bf16(columns, channels), bf16(tokens, channels), bf16(total, channels),
             pltpu.SemaphoreType.DMA((3,)),
         ],
     )(*stay(xproj_weight.T, prefill_x, decode_flat))
-    parts = lax.all_to_all(partial, "tp", 0, 0)
-    copies = call(total_kernel, "total", chunked, [VMEM])(parts)
-    proj = lax.all_to_all(copies, "tp", 0, 0)
+    copies = call(functools.partial(total_kernel, ranks=ranks), "total", flat, [VMEM])(
+        exchange(partial)
+    )
+    proj = exchange(copies)
 
     scan_scratch = [
         f32(tokens, channels), f32(tokens, channels), f32(2 * width, tokens), f32(width, channels)
     ]
     send = call(
         states_kernel, "states", struct((groups, CAP, width, channels)),
-        [SMEM, SMEM, pl.BlockSpec((ranks // 2, per, columns), lambda i: (0, 0, 0))] + [VMEM] * 4,
+        [SMEM, SMEM] + [VMEM] * 5,
         out_specs=ANY,
         scratch=scan_scratch
         + [f32(tokens, width, channels), pltpu.SemaphoreType.DMA((requests,))],

time: 69.8 us -> 67.7 us (0.970)
  blocking collectives: 36.3 us -> 33.6 us
    all_to_all x2, blocking collectives: 36.3 us -> 33.6 us  [exchange(): return lax.all_to_all(chunks, 'tp', 0, 0).reshape(ranks * height, LANES)]
where the time goes in v4:
time: 67.7 us; the launch traced here: 67.4 us
  blocking collectives  33.6 us (50%)
  Pallas kernels  14.2 us (21%)
  starting transfers between devices  10.9 us (16%)
  waiting for transfers between devices  7.85 us (12%)
  between operations  0.74 us (1%)
    all_to_all x2, blocking collectives, exchange(): return lax.all_to_all(chunks, 'tp', 0, 0).reshape(ranks * height, LANES)  33.6 us
    all_to_all x1, starting transfers between devices, local(): recv = lax.all_to_all(send, 'group', 0, 0)  10.9 us
    all_to_all x1, waiting for transfers between devices, local(): recv = lax.all_to_all(send, 'group', 0, 0)  7.85 us
    pallas_call x1, Pallas kernels, local(): call(functools.partial(rest_kernel, groups=groups), 'rest', (struct((toke...  7.74 us
    pallas_call x1, Pallas kernels, local(): call(states_kernel, 'states', struct((groups, CAP, width, channels)), [SM...  2.99 us
    pallas_call x1, Pallas kernels, local(): call(functools.partial(project_kernel, rank=rank), 'project', flat, [ANY]...  1.86 us
    pallas_call x1, Pallas kernels, local(): call(combine_kernel, 'combine', struct((total, channels), jnp.bfloat16),...  1.55 us
  transfers between devices with their start and end apart: 1, of which 1 were waited for; matrix products, arithmetic and copies ran while one was open for 0% of the time, Pallas kernels for 11%

profile of v4, /device:TPU:1, one launch (start us, length us, event | category | flops | bytes accessed | tf_op | source)
XLA Modules:
  0.0 67.4 jit_solution(10498158155014195730)
XLA Ops:
  0.6 0.0 copy-start
  0.6 0.0 copy-start.1
  0.7 0.0 copy-start.2
  0.7 0.0 copy-start.3
  0.7 0.0 copy-start.4
  0.7 0.0 copy-start.5
  0.7 1.9 %project.1 = f32[1088,128]{1,0:T(8,128)S(1)} custom-call(bf16[544,512]{1,0:T(8,128)(2,1)} %bitcast.22, bf16[128,512]{1,0:T(8,128)(2,1)} %x_ref.1, bf16[128,512]{1,0:T(8,128)(2,1)} %bitcast.24), custom_call_target="tpu_custom_call" | custom-call | bytes 1048576 | tf_op jit(solution)/shard_map/project/pallas_call | solution.py:382
  2.6 20.4 %all_to_all.15 = f32[32,17,2,128]{3,2,1,0:T(2,128)S(1)} all-to-all(f32[32,17,2,128]{3,2,1,0:T(2,128)S(1)} %bitcast.16), channel_id=1, replica_groups=mesh['group'=8,'tp'=32] {'tp'}, dimensions={0} | all-to-all | bytes 1114112 | tf_op jit(solution)/shard_map/all_to_all | solution.py:380
  23.0 0.1 total.1
  23.0 13.3 %all_to_all.16 = f32[32,17,2,128]{3,2,1,0:T(2,128)S(1)} all-to-all(f32[32,17,2,128]{3,2,1,0:T(2,128)S(1)} %bitcast.15), channel_id=1, replica_groups=mesh['group'=8,'tp'=32] {'tp'}, dimensions={0} | all-to-all | bytes 1114112 | tf_op jit(solution)/shard_map/all_to_all | solution.py:380
  36.3 0.0 copy-done
  36.3 0.0 copy-done.1
  36.3 0.0 copy-done.2
  36.3 0.0 copy-done.3
  36.3 0.0 copy-done.4
  36.3 0.0 copy-done.5
  36.3 3.0 %states.1 = f32[8,2,16,512]{3,2,1,0:T(8,128)} custom-call(s32[1,8]{1,0:T(1,128)S(1)} %copy-done.4, s32[1,64]{1,0:T(1,128)S(1)} %bitcast.20, f32[1088,128]{1,0:T(8,128)S(1)} %bitcast.12, bf16[128,512]{1,0:T(8,128)(2,1)S(1)} %copy-done.1, bf16[512,512]{1,0:T(8,128)(2,1)S(1)} %copy-done, f32[1,512]{1,0:T(1,128)S(1)} %bitcast.19, f32[16,512]{1,0:T(8,128)S(1)} %copy-done.2), custom_call_target="tpu_custom_call" | custom-call | bytes 1048576 | tf_op jit(solution)/shard_map/states/pallas_call | solution.py:397
  39.3 10.9 %all-to-all-start.2 = ((f32[8,2,16,512]{3,2,1,0:T(8,128)}), f32[8,2,16,512]{3,2,1,0:T(8,128)S(1)}, u32[]{:S(2)}, u32[]{:S(2)}) async-start(f32[8,2,16,512]{3,2,1,0:T(8,128)} %states.1), calls=%async_computation.2 | async-start | bytes 1048576 | tf_op jit(solution)/shard_map/all_to_all | solution.py:404
  50.3 7.7 %rest.1 = (bf16[128,512]{1,0:T(8,128)(2,1)}, f32[128,512]{1,0:T(8,128)S(1)}, f32[16,4,16,512]{3,2,1,0:T(8,128)S(1)}, s32[16]{0:T(128)S(1)}) custom-call(s32[1,8]{1,0:T(1,128)S(1)} %copy-done.4, s32[1,64]{1,0:T(1,128)S(1)} %bitcast.21, f32[1088,128]{1,0:T(8,128)S(1)} %bitcast.13, f32[32,16,512]{2,1,0:T(8,128)} %state_hbm.1, bf16[128,512]{1,0:T(8,128)(2,1)} %bitcast.25, ...), custom_call_target="tpu_custom_call" | custom-call | flops 8000000000 | bytes 1048576 | tf_op jit(solution)/shard_map/rest/pallas_call | solution.py:405
  58.0 7.8 %all-to-all-done.2 = f32[8,2,16,512]{3,2,1,0:T(8,128)S(1)} async-done(((f32[8,2,16,512]{3,2,1,0:T(8,128)}), f32[8,2,16,512]{3,2,1,0:T(8,128)S(1)}, u32[]{:S(2)}, u32[]{:S(2)}) %all-to-all-start.2) | async-done | bytes 524320 | tf_op jit(solution)/shard_map/all_to_all | solution.py:404
  65.9 1.6 %combine.1 = bf16[128,512]{1,0:T(8,128)(2,1)} custom-call(s32[16]{0:T(128)S(1)} %get-tuple-element.7.source_ref, f32[128,512]{1,0:T(8,128)S(1)} %get-tuple-element.8.mixed_ref, f32[16,4,16,512]{3,2,1,0:T(8,128)S(1)} %get-tuple-element.9.unit_ref, f32[16,16,512]{2,1,0:T(8,128)S(1)} %bitcast.17), custom_call_target="tpu_custom_call" | custom-call | bytes 1048576 | tf_op jit(solution)/shard_map/combine/pallas_call | solution.py:429
Async XLA Ops:
  0.6 35.6 %copy-start = (bf16[512,512]{1,0:T(8,128)(2,1)S(1)}, bf16[512,512]{1,0:T(8,128)(2,1)}, u32[]{:S(2)}) copy-start(bf16[512,512]{1,0:T(8,128)(2,1)} %weight_ref.1) | copy-start | bytes 1572868
  0.6 35.6 %copy-start.1 = (bf16[128,512]{1,0:T(8,128)(2,1)S(1)}, bf16[128,512]{1,0:T(8,128)(2,1)}, u32[]{:S(2)}) copy-start(bf16[128,512]{1,0:T(8,128)(2,1)} %x_ref.1) | copy-start | bytes 393220
  0.7 35.6 %copy-start.2 = (f32[16,512]{1,0:T(8,128)S(1)}, f32[16,512]{1,0:T(8,128)}, u32[]{:S(2)}) copy-start(f32[16,512]{1,0:T(8,128)} %alog_ref.1) | copy-start | bytes 98308
  0.7 35.6 %copy-start.3 = (f32[512]{0:T(512)S(1)}, f32[512]{0:T(512)}, u32[]{:S(2)}) copy-start(f32[512]{0:T(512)} %param.21) | copy-start | bytes 6148
  0.7 35.6 %copy-start.4 = (s32[1,8]{1,0:T(1,128)S(1)}, s32[1,8]{1,0:T(1,128)}, u32[]{:S(2)}) copy-start(s32[1,8]{1,0:T(1,128)} %lengths_ref.3) | copy-start | bytes 100
  0.7 35.6 %copy-start.5 = (s32[64,1]{0,1:T(1,128)S(1)}, s32[64,1]{0,1:T(1,128)}, u32[]{:S(2)}) copy-start(s32[64,1]{0,1:T(1,128)} %param.15) | copy-start | bytes 772
  39.3 26.5 %all-to-all-start.2 = ((f32[8,2,16,512]{3,2,1,0:T(8,128)}), f32[8,2,16,512]{3,2,1,0:T(8,128)S(1)}, u32[]{:S(2)}, u32[]{:S(2)}) async-start(f32[8,2,16,512]{3,2,1,0:T(8,128)} %states.1), calls=%async_computation.2 | async-start | bytes 1048576 | tf_op jit(solution)/shard_map/all_to_all | solution.py:404

commit v5 on v4

--- a/solution.py
+++ b/solution.py
@@ -213,8 +213,10 @@
 
 def states_kernel(
     lengths_ref, routes_ref, proj_ref, x_ref, weight_ref, bias_ref, alog_ref,
-    send_ref, size_ref, force_ref, vec_ref, rates_ref, hist_ref, sems,
+    *rest,
 ):
+    send_refs, (size_ref, force_ref, vec_ref, rates_ref, hist_ref, send_ref) = rest[:-6], rest[-6:]
+    chips = len(send_refs)
     requests = lengths_ref.shape[1]
     group = lax.axis_index("group")
     ends = prepare_scan(
@@ -223,17 +225,15 @@
     )
     scan(size_ref, force_ref, vec_ref, rates_ref, None, None, hist_ref)
     dests = [routes_ref[0, group * requests + k] for k in range(requests)]
-    copies = []
     for k in range(requests):
         lane = jnp.int32(0)
         for j in range(k):
             lane = lane + (dests[j] == dests[k]).astype(jnp.int32)
-        copies.append(
-            pltpu.make_async_copy(hist_ref.at[ends[k]], send_ref.at[dests[k], lane], sems.at[k])
-        )
-        copies[-1].start()
-    for copy in copies:
-        copy.wait()
+        ahead = lax.rem(dests[k] // 2 - group // 2 + chips, chips)
+        other = lax.rem(dests[k] + group, 2)
+        send_ref[ahead, other, lane] = hist_ref[ends[k]]
+    for chip in range(chips):
+        send_refs[chip][...] = send_ref[chip]
 
 
 def rest_kernel(
@@ -275,7 +275,8 @@
 
             @pl.when(ours)
             def _(g=g, slot=slot, lane=lane):
-                source_ref[slot] = g * CAP + lane
+                behind = lax.rem(me // 2 - g // 2 + groups // 2, groups // 2)
+                source_ref[slot] = (behind * 2 + lax.rem(me + g, 2)) * CAP + lane
 
             slot = slot + ours.astype(jnp.int32)
             lane = lane + ours.astype(jnp.int32)
@@ -338,8 +339,17 @@
     out_ref[...] = (mixed * silu(prefill_gate_ref[...].astype(jnp.float32))).astype(out_ref.dtype)
 
 
-def combine_kernel(source_ref, mixed_ref, unit_ref, recv_ref, out_ref):
+def pass_on_kernel(source_ref, *refs):
+    for i, ref in enumerate(refs[:-1]):
+        refs[-1][i] = ref[1]
+
+
+def combine_kernel(source_ref, mixed_ref, unit_ref, swapped_ref, *rest):
+    out_ref, recv_ref = rest[-2:]
     reach, steps = unit_ref.shape[:2]
+    for i, ref in enumerate(rest[:-2]):
+        recv_ref[2 * i * CAP : (2 * i + 1) * CAP] = ref[0]
+        recv_ref[(2 * i + 1) * CAP : (2 * i + 2) * CAP] = swapped_ref[i]
     rows = mixed_ref.shape[0] // steps
     added = [[] for _ in range(steps)]
     for n in range(reach):
@@ -394,14 +404,24 @@
     scan_scratch = [
         f32(tokens, channels), f32(tokens, channels), f32(2 * width, tokens), f32(width, channels)
     ]
+    chips = groups // 2
     send = call(
-        states_kernel, "states", struct((groups, CAP, width, channels)),
+        states_kernel, "states", (struct((2, CAP, width, channels)),) * chips,
         [SMEM, SMEM] + [VMEM] * 5,
-        out_specs=ANY,
+        out_specs=(VMEM,) * chips,
         scratch=scan_scratch
-        + [f32(tokens, width, channels), pltpu.SemaphoreType.DMA((requests,))],
+        + [f32(tokens, width, channels), f32(chips, 2, CAP, width, channels)],
     )(lengths, routes, proj, prefill_x, dt_weight, bias, a_log)
-    recv = lax.all_to_all(send, "group", 0, 0)
+
+    def move(states, ahead, other):
+        pairs = [
+            (g, (g // 2 + ahead) % chips * 2 + (g + other) % 2) for g in range(groups)
+        ]
+        return lax.ppermute(states, "group", pairs)
+
+    arrived = [send[0]] + [None] * (chips - 1)
+    for ahead in sorted(range(1, chips), key=lambda d: min(d, chips - d)):
+        arrived[ahead] = move(send[ahead], ahead, 0)
     prefill_out, mixed, unit, source = call(
         functools.partial(rest_kernel, groups=groups), "rest",
         (
@@ -426,9 +446,18 @@
             prefill_gate,
         ),
     )
+    swapped = move(
+        call(
+            pass_on_kernel, "pass_on", struct((chips, CAP, width, channels)),
+            [SMEM] + [VMEM] * chips,
+        )(source, *arrived),
+        0, 1,
+    )
     decode_out = call(
-        combine_kernel, "combine", struct((total, channels), jnp.bfloat16), [SMEM] + [VMEM] * 3
-    )(source, mixed, unit, recv.reshape(reach, width, channels))
+        combine_kernel, "combine", struct((total, channels), jnp.bfloat16),
+        [SMEM] + [VMEM] * (3 + chips),
+        scratch=[f32(reach, width, channels)],
+    )(source, mixed, unit, swapped, *arrived)
     return prefill_out, decode_out.reshape(steps, rows, channels)
 
 

time: 67.7 us -> 63.9 us (0.944)
  waiting for transfers between devices: 7.85 us -> 2.69 us
  starting transfers between devices: 10.9 us -> 12.4 us
    ppermute x0 -> x4, starting transfers between devices: none -> 12.4 us  [move(): return lax.ppermute(states, 'group', pairs)]
    all_to_all x1 -> x0, starting transfers between devices: 10.9 us -> none  [local(): recv = lax.all_to_all(send, 'group', 0, 0)]
    all_to_all x1 -> x0, waiting for transfers between devices: 7.85 us -> none  [local(): recv = lax.all_to_all(send, 'group', 0, 0)]
    ppermute x0 -> x4, waiting for transfers between devices: none -> 2.69 us  [move(): return lax.ppermute(states, 'group', pairs)]
    pallas_call x1 -> x2, Pallas kernels: 2.99 us -> 2.9 us  [the longest x1 2.34 us: local(): call(states_kernel, 'states', (struct((2, CAP, width, channels)),) * chip...]
  transfers between devices with their start and end apart: 1 -> 4, of which waited for: 1 -> 2; matrix products, arithmetic and copies ran while one was open for 0% -> 0% of each run, Pallas kernels for 11% -> 12%
where the time goes in v5:
time: 63.9 us; the launch traced here: 63.7 us
  blocking collectives  33.6 us (53%)
  Pallas kernels  14.2 us (22%)
  starting transfers between devices  12.4 us (19%)
  waiting for transfers between devices  2.69 us (4%)
  between operations  0.76 us (1%)
    all_to_all x2, blocking collectives, exchange(): return lax.all_to_all(chunks, 'tp', 0, 0).reshape(ranks * height, LANES)  33.6 us
    ppermute x4, starting transfers between devices, move(): return lax.ppermute(states, 'group', pairs)  12.4 us
    pallas_call x1, Pallas kernels, local(): call(functools.partial(rest_kernel, groups=groups), 'rest', (struct((toke...  7.76 us
    ppermute x4, waiting for transfers between devices, move(): return lax.ppermute(states, 'group', pairs)  2.69 us
    pallas_call x1, Pallas kernels, local(): call(states_kernel, 'states', (struct((2, CAP, width, channels)),) * chip...  2.34 us
    pallas_call x1, Pallas kernels, local(): call(functools.partial(project_kernel, rank=rank), 'project', flat, [ANY]...  1.86 us
    pallas_call x1, Pallas kernels, local(): call(combine_kernel, 'combine', struct((total, channels), jnp.bfloat16),...  1.61 us
  transfers between devices with their start and end apart: 4, of which 2 were waited for; matrix products, arithmetic and copies ran while one was open for 0% of the time, Pallas kernels for 12%

profile of v5, /device:TPU:1, one launch (start us, length us, event | category | flops | bytes accessed | tf_op | source)
XLA Modules:
  0.0 63.7 jit_solution(320985067664532234)
XLA Ops:
  0.6 0.0 copy-start
  0.6 0.0 copy-start.1
  0.7 0.0 copy-start.2
  0.7 0.0 copy-start.3
  0.7 0.0 copy-start.4
  0.7 0.0 copy-start.5
  0.7 1.9 %project.1 = f32[1088,128]{1,0:T(8,128)S(1)} custom-call(bf16[544,512]{1,0:T(8,128)(2,1)} %bitcast.20, bf16[128,512]{1,0:T(8,128)(2,1)} %x_ref.1, bf16[128,512]{1,0:T(8,128)(2,1)} %bitcast.22), custom_call_target="tpu_custom_call" | custom-call | bytes 1048576 | tf_op jit(solution)/shard_map/project/pallas_call | solution.py:392
  2.6 20.4 %all_to_all.10 = f32[32,17,2,128]{3,2,1,0:T(2,128)S(1)} all-to-all(f32[32,17,2,128]{3,2,1,0:T(2,128)S(1)} %bitcast.15), channel_id=1, replica_groups=mesh['group'=8,'tp'=32] {'tp'}, dimensions={0} | all-to-all | bytes 1114112 | tf_op jit(solution)/shard_map/all_to_all | solution.py:390
  23.0 0.1 total.1
  23.0 13.3 %all_to_all.11 = f32[32,17,2,128]{3,2,1,0:T(2,128)S(1)} all-to-all(f32[32,17,2,128]{3,2,1,0:T(2,128)S(1)} %bitcast.14), channel_id=1, replica_groups=mesh['group'=8,'tp'=32] {'tp'}, dimensions={0} | all-to-all | bytes 1114112 | tf_op jit(solution)/shard_map/all_to_all | solution.py:390
  36.3 0.0 copy-done
  36.3 0.0 copy-done.1
  36.3 0.0 copy-done.2
  36.3 0.0 copy-done.3
  36.3 0.0 copy-done.4
  36.3 0.0 copy-done.5
  36.3 2.3 %states.1 = (f32[2,2,16,512]{3,2,1,0:T(8,128)S(1)}, f32[2,2,16,512]{3,2,1,0:T(8,128)S(1)}, f32[2,2,16,512]{3,2,1,0:T(8,128)S(1)}, f32[2,2,16,512]{3,2,1,0:T(8,128)S(1)}) custom-call(s32[1,8]{1,0:T(1,128)S(1)} %copy-done.4, s32[1,64]{1,0:T(1,128)S(1)} %bitcast.18, f32[1088,128]{1,0:T(8,128)S(1)} %bitcast.11, bf16[128,512]{1,0:T(8,128)(2,1)S(1)} %copy-done.1, ...), custom_call_target="tpu_custom_call" | custom-call | bytes 1048576 | tf_op jit(solution)/shard_map/states/pallas_call | solution.py:408
  38.7 3.1 %collective-permute-start = (f32[2,2,16,512]{3,2,1,0:T(8,128)S(1)}, f32[2,2,16,512]{3,2,1,0:T(8,128)S(1)}, u32[]{:S(2)}, u32[]{:S(2)}) collective-permute-start(f32[2,2,16,512]{3,2,1,0:T(8,128)S(1)} %get-tuple-element.15), channel_id=1, source_target_pairs={{0,64},{32,96},{64,128},{96,160},{128,192},{160,224},{192,0},{224,... | collective-permute-start | bytes 393224 | tf_op jit(solution)/shard_map/ppermute | solution.py:420
  41.7 4.2 %collective-permute-start.1 = (f32[2,2,16,512]{3,2,1,0:T(8,128)S(1)}, f32[2,2,16,512]{3,2,1,0:T(8,128)S(1)}, u32[]{:S(2)}, u32[]{:S(2)}) collective-permute-start(f32[2,2,16,512]{3,2,1,0:T(8,128)S(1)} %get-tuple-element.16), channel_id=1, source_target_pairs={{0,128},{32,160},{64,192},{96,224},{128,0},{160,32},{192,64},{224,... | collective-permute-start | bytes 393224 | tf_op jit(solution)/shard_map/ppermute | solution.py:420
  45.9 2.4 %collective-permute-start.2 = (f32[2,2,16,512]{3,2,1,0:T(8,128)S(1)}, f32[2,2,16,512]{3,2,1,0:T(8,128)S(1)}, u32[]{:S(2)}, u32[]{:S(2)}) collective-permute-start(f32[2,2,16,512]{3,2,1,0:T(8,128)S(1)} %get-tuple-element.17), channel_id=1, source_target_pairs={{0,192},{32,224},{64,0},{96,32},{128,64},{160,96},{192,128},{224,1... | collective-permute-start | bytes 393224 | tf_op jit(solution)/shard_map/ppermute | solution.py:420
  48.3 7.8 %rest.1 = (bf16[128,512]{1,0:T(8,128)(2,1)}, f32[128,512]{1,0:T(8,128)S(1)}, f32[16,4,16,512]{3,2,1,0:T(8,128)S(1)}, s32[16]{0:T(128)S(1)}) custom-call(s32[1,8]{1,0:T(1,128)S(1)} %copy-done.4, s32[1,64]{1,0:T(1,128)S(1)} %bitcast.19, f32[1088,128]{1,0:T(8,128)S(1)} %bitcast.12, f32[32,16,512]{2,1,0:T(8,128)} %state_hbm.1, bf16[128,512]{1,0:T(8,128)(2,1)} %bitcast.23, ...), custom_call_target="tpu_custom_call" | custom-call | flops 8000000000 | bytes 1048576 | tf_op jit(solution)/shard_map/rest/pallas_call | solution.py:425
  56.1 0.0 collective-permute-done.refs_1_.rest_1_
  56.1 0.0 collective-permute-done.1.refs_2_.rest_2_
  56.1 1.5 %collective-permute-done.2.refs_3_.rest_3_ = f32[2,2,16,512]{3,2,1,0:T(8,128)S(1)} collective-permute-done((f32[2,2,16,512]{3,2,1,0:T(8,128)S(1)}, f32[2,2,16,512]{3,2,1,0:T(8,128)S(1)}, u32[]{:S(2)}, u32[]{:S(2)}) %collective-permute-start.2) | collective-permute-done | bytes 131104 | tf_op jit(solution)/shard_map/ppermute | solution.py:420
  57.6 0.6 pass_on.1
  58.2 2.8 %collective-permute-start.3 = (f32[4,2,16,512]{3,2,1,0:T(8,128)S(1)}, f32[4,2,16,512]{3,2,1,0:T(8,128)S(1)}, u32[]{:S(2)}, u32[]{:S(2)}) collective-permute-start(f32[4,2,16,512]{3,2,1,0:T(8,128)S(1)} %pass_on.1), channel_id=1, source_target_pairs={{0,32},{32,0},{64,96},{96,64},{128,160},{160,128},{192,224},{224,1... | collective-permute-start | bytes 786440 | tf_op jit(solution)/shard_map/ppermute | solution.py:420
  61.0 1.2 %collective-permute-done.3.swapped_ref = f32[4,2,16,512]{3,2,1,0:T(8,128)S(1)} collective-permute-done((f32[4,2,16,512]{3,2,1,0:T(8,128)S(1)}, f32[4,2,16,512]{3,2,1,0:T(8,128)S(1)}, u32[]{:S(2)}, u32[]{:S(2)}) %collective-permute-start.3) | collective-permute-done | bytes 262176 | tf_op jit(solution)/shard_map/ppermute | solution.py:420
  62.1 1.6 %combine.1 = bf16[128,512]{1,0:T(8,128)(2,1)} custom-call(s32[16]{0:T(128)S(1)} %get-tuple-element.11.source_ref, f32[128,512]{1,0:T(8,128)S(1)} %get-tuple-element.12.mixed_ref, f32[16,4,16,512]{3,2,1,0:T(8,128)S(1)} %get-tuple-element.13.unit_ref, f32[4,2,16,512]{3,2,1,0:T(8,128)S(1)} %collective-permute-done.3.swapped_ref, ...), custom_call_target="tpu_custom_call" | custom-call | bytes 1048576 | tf_op jit(solution)/shard_map/combine/pallas_call | solution.py:456
Async XLA Ops:
  0.6 35.6 %copy-start = (bf16[512,512]{1,0:T(8,128)(2,1)S(1)}, bf16[512,512]{1,0:T(8,128)(2,1)}, u32[]{:S(2)}) copy-start(bf16[512,512]{1,0:T(8,128)(2,1)} %weight_ref.1) | copy-start | bytes 1572868
  0.6 35.6 %copy-start.1 = (bf16[128,512]{1,0:T(8,128)(2,1)S(1)}, bf16[128,512]{1,0:T(8,128)(2,1)}, u32[]{:S(2)}) copy-start(bf16[128,512]{1,0:T(8,128)(2,1)} %x_ref.1) | copy-start | bytes 393220
  0.7 35.6 %copy-start.2 = (f32[16,512]{1,0:T(8,128)S(1)}, f32[16,512]{1,0:T(8,128)}, u32[]{:S(2)}) copy-start(f32[16,512]{1,0:T(8,128)} %alog_ref.1) | copy-start | bytes 98308
  0.7 35.6 %copy-start.3 = (f32[512]{0:T(512)S(1)}, f32[512]{0:T(512)}, u32[]{:S(2)}) copy-start(f32[512]{0:T(512)} %param.21) | copy-start | bytes 6148
  0.7 35.6 %copy-start.4 = (s32[1,8]{1,0:T(1,128)S(1)}, s32[1,8]{1,0:T(1,128)}, u32[]{:S(2)}) copy-start(s32[1,8]{1,0:T(1,128)} %lengths_ref.3) | copy-start | bytes 100
  0.7 35.6 %copy-start.5 = (s32[64,1]{0,1:T(1,128)S(1)}, s32[64,1]{0,1:T(1,128)}, u32[]{:S(2)}) copy-start(s32[64,1]{0,1:T(1,128)} %param.15) | copy-start | bytes 772
  38.7 17.4 %collective-permute-start = (f32[2,2,16,512]{3,2,1,0:T(8,128)S(1)}, f32[2,2,16,512]{3,2,1,0:T(8,128)S(1)}, u32[]{:S(2)}, u32[]{:S(2)}) collective-permute-start(f32[2,2,16,512]{3,2,1,0:T(8,128)S(1)} %get-tuple-element.15), channel_id=1, source_target_pairs={{0,64},{32,96},{64,128},{96,160},{128,192},{160,224},{192,0},{224,... | collective-permute-start | bytes 393224 | tf_op jit(solution)/shard_map/ppermute | solution.py:420
  41.7 14.4 %collective-permute-start.1 = (f32[2,2,16,512]{3,2,1,0:T(8,128)S(1)}, f32[2,2,16,512]{3,2,1,0:T(8,128)S(1)}, u32[]{:S(2)}, u32[]{:S(2)}) collective-permute-start(f32[2,2,16,512]{3,2,1,0:T(8,128)S(1)} %get-tuple-element.16), channel_id=1, source_target_pairs={{0,128},{32,160},{64,192},{96,224},{128,0},{160,32},{192,64},{224,... | collective-permute-start | bytes 393224 | tf_op jit(solution)/shard_map/ppermute | solution.py:420
  45.9 11.7 %collective-permute-start.2 = (f32[2,2,16,512]{3,2,1,0:T(8,128)S(1)}, f32[2,2,16,512]{3,2,1,0:T(8,128)S(1)}, u32[]{:S(2)}, u32[]{:S(2)}) collective-permute-start(f32[2,2,16,512]{3,2,1,0:T(8,128)S(1)} %get-tuple-element.17), channel_id=1, source_target_pairs={{0,192},{32,224},{64,0},{96,32},{128,64},{160,96},{192,128},{224,1... | collective-permute-start | bytes 393224 | tf_op jit(solution)/shard_map/ppermute | solution.py:420
  58.2 3.9 %collective-permute-start.3 = (f32[4,2,16,512]{3,2,1,0:T(8,128)S(1)}, f32[4,2,16,512]{3,2,1,0:T(8,128)S(1)}, u32[]{:S(2)}, u32[]{:S(2)}) collective-permute-start(f32[4,2,16,512]{3,2,1,0:T(8,128)S(1)} %pass_on.1), channel_id=1, source_target_pairs={{0,32},{32,0},{64,96},{96,64},{128,160},{160,128},{192,224},{224,1... | collective-permute-start | bytes 786440 | tf_op jit(solution)/shard_map/ppermute | solution.py:420

commit v6 on v5

--- a/solution.py
+++ b/solution.py
@@ -97,20 +97,21 @@
         (weight_hbm, prefill_hbm, decode_hbm), (weight_ref, prefill_ref, decode_ref), sems
     )
     count = weight_ref.shape[0] - rank
-    half = count // 2
-    copies[0].wait()
-    for which, ref in enumerate((prefill_ref, decode_ref)):
-        copies[which + 1].wait()
-        values = ref[...]
-        low = lax.dot_general(
-            values, weight_ref[:rank], (((1,), (1,)), ((), ())), preferred_element_type=jnp.float32
-        )
-        for j in range(half):
-            for tile, cols in enumerate(tiles_of(rank)):
-                out_ref[low_rows(rank, half * which + j, tile), :] = low[8 * j : 8 * j + 8, cols]
-        out_ref[vector_rows(rank, count, which), :] = lax.dot_general(
-            weight_ref[rank:], values, (((1,), (1,)), ((), ())), preferred_element_type=jnp.float32
-        )
+    for copy in copies:
+        copy.wait()
+    values = jnp.concatenate([prefill_ref[...], decode_ref[...]], axis=0)
+    low = lax.dot_general(
+        values, weight_ref[:rank], (((1,), (1,)), ((), ())), preferred_element_type=jnp.float32
+    )
+    for j in range(count):
+        for tile, cols in enumerate(tiles_of(rank)):
+            out_ref[low_rows(rank, j, tile), :] = low[8 * j : 8 * j + 8, cols]
+    vectors = lax.dot_general(
+        weight_ref[rank:], values, (((1,), (1,)), ((), ())), preferred_element_type=jnp.float32
+    )
+    rows = prefill_ref.shape[0]
+    for which in range(2):
+        out_ref[vector_rows(rank, count, which), :] = vectors[:, which * rows : (which + 1) * rows]
 
 
 def total_kernel(parts_ref, out_ref, *, ranks):
@@ -157,13 +158,16 @@
             part_ref[tile, at : at + 8, :] = fold(readout * hidden[tile])
 
 
-def prepare_scan(lengths_ref, proj_ref, x_ref, weight_ref, bias_ref, alog_ref, size_ref, force_ref, vec_ref, rates_ref):
+def prepare_scan(table, lengths_ref, proj_ref, x_ref, weight_ref, bias_ref, alog_ref, size_ref, force_ref, vec_ref, rates_ref):
     tokens, channels = x_ref.shape
     rank = weight_ref.shape[0]
     count = vec_ref.shape[0]
     low = low_part(proj_ref, rank, count // 2, 0)
     size = step_sizes(low, weight_ref, bias_ref)
     force_ref[...] = size * x_ref[...].astype(jnp.float32)
+    vec_ref[...] = proj_ref[vector_rows(rank, count, 0), :]
+    rates_ref[...] = -LOG2E * jnp.exp(alog_ref[...])
+    table.wait()
     position = lax.broadcasted_iota(jnp.int32, (tokens, LANES), 0)
     first = position == 0
     begin = jnp.int32(0)
@@ -175,8 +179,6 @@
     reset = jnp.where(first, jnp.float32(FAR), jnp.float32(0.0))
     for cols in tiles_of(channels):
         size_ref[:, cols] = size[:, cols] + reset
-    vec_ref[...] = proj_ref[vector_rows(rank, count, 0), :]
-    rates_ref[...] = -LOG2E * jnp.exp(alog_ref[...])
     return ends
 
 
@@ -212,18 +214,21 @@
 
 
 def states_kernel(
-    lengths_ref, routes_ref, proj_ref, x_ref, weight_ref, bias_ref, alog_ref,
+    lengths_any, routes_any, proj_ref, x_ref, weight_ref, bias_ref, alog_ref,
     *rest,
 ):
-    send_refs, (size_ref, force_ref, vec_ref, rates_ref, hist_ref, send_ref) = rest[:-6], rest[-6:]
+    send_refs, rest = rest[:-9], rest[-9:]
+    lengths_ref, routes_ref, size_ref, force_ref, vec_ref, rates_ref, hist_ref, send_ref, sems = rest
+    tables = fetch((lengths_any, routes_any), (lengths_ref, routes_ref), sems)
     chips = len(send_refs)
     requests = lengths_ref.shape[1]
     group = lax.axis_index("group")
     ends = prepare_scan(
-        lengths_ref, proj_ref, x_ref, weight_ref, bias_ref, alog_ref, size_ref, force_ref, vec_ref,
+        tables[0], lengths_ref, proj_ref, x_ref, weight_ref, bias_ref, alog_ref, size_ref, force_ref, vec_ref,
         rates_ref,
     )
     scan(size_ref, force_ref, vec_ref, rates_ref, None, None, hist_ref)
+    tables[1].wait()
     dests = [routes_ref[0, group * requests + k] for k in range(requests)]
     for k in range(requests):
         lane = jnp.int32(0)
@@ -237,36 +242,47 @@
 
 
 def rest_kernel(
-    lengths_ref, routes_ref, proj_ref,
-    state_hbm, decode_x_hbm, decode_gate_hbm, weight_hbm, alog_hbm, bias_hbm, skip_hbm,
-    prefill_x_hbm, prefill_gate_hbm,
-    out_ref, mixed_ref, unit_ref, source_ref,
-    state_ref, decode_x_ref, decode_gate_ref, weight_ref, alog_ref, bias_ref, skip_ref,
-    prefill_x_ref, prefill_gate_ref,
-    size_ref, force_ref, act_ref, sum_ref, part_ref, vec_ref, rates_ref, sems, *, groups,
+    proj_ref, weight_ref, alog_ref, bias_ref, prefill_x_ref,
+    lengths_any, routes_any, prefill_gate_hbm, skip_hbm, decode_x_hbm, decode_gate_hbm, state_hbm,
+    out_ref, mixed_ref, unit_ref, row_ref,
+    lengths_ref, routes_ref, prefill_gate_ref, skip_ref, decode_x_ref, decode_gate_ref, state_ref,
+    source_ref, size_ref, force_ref, act_ref, sum_ref, part_ref, vec_ref, rates_ref, sems, *, groups,
 ):
     copies = fetch(
         (
-            weight_hbm, alog_hbm, bias_hbm, skip_hbm, decode_x_hbm, decode_gate_hbm, state_hbm,
-            prefill_x_hbm, prefill_gate_hbm,
+            lengths_any, routes_any, prefill_gate_hbm, skip_hbm, decode_x_hbm, decode_gate_hbm,
+            state_hbm,
         ),
         (
-            weight_ref, alog_ref, bias_ref, skip_ref, decode_x_ref, decode_gate_ref, state_ref,
-            prefill_x_ref, prefill_gate_ref,
+            lengths_ref, routes_ref, prefill_gate_ref, skip_ref, decode_x_ref, decode_gate_ref,
+            state_ref,
         ),
         sems,
     )
     total, channels = decode_x_ref.shape
     rows, width = state_ref.shape[:2]
     steps = total // rows
-    reach = unit_ref.shape[0]
+    reach = source_ref.shape[0]
     tiles = tiles_of(channels)
     rank = weight_ref.shape[0]
     count = vec_ref.shape[0]
     requests = lengths_ref.shape[1]
     me = lax.axis_index("group")
+
+    prepare_scan(
+        copies[0], lengths_ref, proj_ref, prefill_x_ref, weight_ref, bias_ref, alog_ref, size_ref,
+        force_ref, vec_ref, rates_ref,
+    )
+    scan(size_ref, force_ref, vec_ref, rates_ref, sum_ref, part_ref, None)
+    copies[2].wait()
+    copies[3].wait()
+    mixed = sum_ref[...] + skip_ref[...] * prefill_x_ref[...].astype(jnp.float32)
+    out_ref[...] = (mixed * silu(prefill_gate_ref[...].astype(jnp.float32))).astype(out_ref.dtype)
+
+    copies[1].wait()
     for n in range(reach):
-        source_ref[n] = -1
+        source_ref[n] = reach
+        row_ref[n] = -1
     slot = jnp.int32(0)
     for g in range(groups):
         lane = jnp.int32(0)
@@ -276,20 +292,20 @@
             @pl.when(ours)
             def _(g=g, slot=slot, lane=lane):
                 behind = lax.rem(me // 2 - g // 2 + groups // 2, groups // 2)
-                source_ref[slot] = (behind * 2 + lax.rem(me + g, 2)) * CAP + lane
+                source = (behind * 2 + lax.rem(me + g, 2)) * CAP + lane
+                source_ref[slot] = source
+                row_ref[source] = slot
 
             slot = slot + ours.astype(jnp.int32)
             lane = lane + ours.astype(jnp.int32)
 
-    for copy in copies[:5]:
-        copy.wait()
+    copies[4].wait()
+    copies[5].wait()
     size = step_sizes(low_part(proj_ref, rank, count // 2, 1), weight_ref, bias_ref)
     values = decode_x_ref[...].astype(jnp.float32)
     size_ref[...] = size
     force_ref[...] = size * values
     vec_ref[...] = proj_ref[vector_rows(rank, count, 1), :]
-    rates_ref[...] = -LOG2E * jnp.exp(alog_ref[...])
-    copies[5].wait()
     act_ref[...] = silu(decode_gate_ref[...].astype(jnp.float32))
     copies[6].wait()
 
@@ -303,8 +319,8 @@
         for i in range(8):
             hidden = [state_ref[base + i, :, cols] for cols in tiles]
             if units:
-                taken = source_ref[base + i] >= 0
-                hidden = [jnp.where(taken, 0.0, start) for start in hidden]
+                source = source_ref[base + i]
+                hidden = [jnp.where(source < reach, 0.0, start) for start in hidden]
             summed = None
             for s in range(steps):
                 inject = jnp.broadcast_to(vectors[s][:width, i : i + 1], (width, LANES))
@@ -317,7 +333,7 @@
                 if units:
                     summed = row if s == 0 else summed + row
                     for cols in tiles:
-                        unit_ref[base + i, s, :, cols] = (
+                        unit_ref[source, s, :, cols] = (
                             readout * acts[s][i : i + 1, cols]
                         ) * jnp.exp2(summed[:, cols] * rates_ref[:, cols])
         for s in range(steps):
@@ -328,41 +344,31 @@
     lax.fori_loop(reach // 8, rows // 8, functools.partial(block, units=False), 0)
     mixed_ref[...] = (sum_ref[...] + skip_ref[...] * values) * act_ref[...]
 
-    copies[7].wait()
-    prepare_scan(
-        lengths_ref, proj_ref, prefill_x_ref, weight_ref, bias_ref, alog_ref, size_ref, force_ref,
-        vec_ref, rates_ref,
-    )
-    scan(size_ref, force_ref, vec_ref, rates_ref, sum_ref, part_ref, None)
-    copies[8].wait()
-    mixed = sum_ref[...] + skip_ref[...] * prefill_x_ref[...].astype(jnp.float32)
-    out_ref[...] = (mixed * silu(prefill_gate_ref[...].astype(jnp.float32))).astype(out_ref.dtype)
-
-
-def pass_on_kernel(source_ref, *refs):
+
+def pass_on_kernel(mixed_ref, *refs):
     for i, ref in enumerate(refs[:-1]):
         refs[-1][i] = ref[1]
 
 
-def combine_kernel(source_ref, mixed_ref, unit_ref, swapped_ref, *rest):
-    out_ref, recv_ref = rest[-2:]
-    reach, steps = unit_ref.shape[:2]
-    for i, ref in enumerate(rest[:-2]):
-        recv_ref[2 * i * CAP : (2 * i + 1) * CAP] = ref[0]
-        recv_ref[(2 * i + 1) * CAP : (2 * i + 2) * CAP] = swapped_ref[i]
+def combine_kernel(row_any, mixed_ref, unit_ref, swapped_ref, *rest):
+    here_refs, (out_ref, row_ref, sum_ref, sems) = rest[:-4], rest[-4:]
+    (table,) = fetch((row_any,), (row_ref,), sems)
+    steps = unit_ref.shape[1]
     rows = mixed_ref.shape[0] // steps
-    added = [[] for _ in range(steps)]
-    for n in range(reach):
-        source = source_ref[n]
-        state = jnp.where(source >= 0, recv_ref[jnp.maximum(source, 0)], 0.0)
-        for s in range(steps):
-            added[s].append(jnp.sum(unit_ref[n, s] * state, axis=0, keepdims=True))
-    for s in range(steps):
-        first, last = s * rows, (s + 1) * rows
-        out_ref[first : first + reach, :] = (
-            mixed_ref[first : first + reach, :] + jnp.concatenate(added[s], axis=0)
-        ).astype(out_ref.dtype)
-        out_ref[first + reach : last, :] = mixed_ref[first + reach : last, :].astype(out_ref.dtype)
+    sum_ref[...] = mixed_ref[...]
+    added = []
+    for i, ref in enumerate(here_refs):
+        for c in range(2 * CAP):
+            state = ref[0, c] if c < CAP else swapped_ref[i, c - CAP]
+            for s in range(steps):
+                terms = unit_ref[2 * CAP * i + c, s] * state
+                added.append(jnp.sum(terms, axis=0, keepdims=True))
+    table.wait()
+    for i, term in enumerate(added):
+        row = row_ref[i // steps]
+        at = pl.ds(i % steps * rows + jnp.maximum(row, 0), 1)
+        sum_ref[at, :] = sum_ref[at, :] + jnp.where(row >= 0, term, 0.0)
+    out_ref[...] = sum_ref[...].astype(out_ref.dtype)
 
 
 def local(
@@ -401,16 +407,20 @@
     )
     proj = exchange(copies)
 
+    tables = [pltpu.SMEM(lengths.shape, jnp.int32), pltpu.SMEM(routes.shape, jnp.int32)]
     scan_scratch = [
         f32(tokens, channels), f32(tokens, channels), f32(2 * width, tokens), f32(width, channels)
     ]
     chips = groups // 2
     send = call(
         states_kernel, "states", (struct((2, CAP, width, channels)),) * chips,
-        [SMEM, SMEM] + [VMEM] * 5,
+        [ANY, ANY] + [VMEM] * 5,
         out_specs=(VMEM,) * chips,
-        scratch=scan_scratch
-        + [f32(tokens, width, channels), f32(chips, 2, CAP, width, channels)],
+        scratch=tables + scan_scratch
+        + [
+            f32(tokens, width, channels), f32(chips, 2, CAP, width, channels),
+            pltpu.SemaphoreType.DMA((2,)),
+        ],
     )(lengths, routes, proj, prefill_x, dt_weight, bias, a_log)
 
     def move(states, ahead, other):
@@ -422,42 +432,41 @@
     arrived = [send[0]] + [None] * (chips - 1)
     for ahead in sorted(range(1, chips), key=lambda d: min(d, chips - d)):
         arrived[ahead] = move(send[ahead], ahead, 0)
-    prefill_out, mixed, unit, source = call(
+    prefill_out, mixed, unit, row_of = call(
         functools.partial(rest_kernel, groups=groups), "rest",
         (
             struct((tokens, channels), jnp.bfloat16), struct((total, channels)),
-            struct((reach, steps, width, channels)), struct((reach,), jnp.int32),
+            struct((reach + 1, steps, width, channels)), struct((reach,), jnp.int32),
         ),
-        [SMEM, SMEM, VMEM] + [ANY] * 9,
+        [VMEM] * 5 + [ANY] * 7,
         out_specs=(VMEM, VMEM, VMEM, SMEM),
-        scratch=[
-            f32(rows, width, channels), bf16(total, channels), bf16(total, channels),
-            bf16(*dt_weight.shape), f32(width, channels), f32(1, channels), f32(1, channels),
-            bf16(tokens, channels), bf16(tokens, channels),
+        scratch=tables + [
+            bf16(tokens, channels), f32(1, channels), bf16(total, channels),
+            bf16(total, channels), f32(rows, width, channels),
+            pltpu.SMEM((reach,), jnp.int32),
             f32(total, channels), f32(total, channels), f32(total, channels),
-            f32(total, channels), f32(channels // LANES, steps * 64, LANES), f32(2 * width, total),
-            f32(width, channels), pltpu.SemaphoreType.DMA((9,)),
+            f32(total, channels), f32(channels // LANES, steps * 64, LANES),
+            f32(2 * width, total), f32(width, channels), pltpu.SemaphoreType.DMA((7,)),
         ],
         flops=8 * 10**9,
     )(
-        lengths, routes, proj,
-        *stay(
-            cached_state, decode_flat, gate_flat, dt_weight, a_log, bias, skip, prefill_x,
-            prefill_gate,
-        ),
+        proj, dt_weight, a_log, bias, prefill_x, lengths, routes,
+        *stay(prefill_gate, skip, decode_flat, gate_flat, cached_state),
     )
     swapped = move(
         call(
             pass_on_kernel, "pass_on", struct((chips, CAP, width, channels)),
-            [SMEM] + [VMEM] * chips,
-        )(source, *arrived),
+            [ANY] + [VMEM] * chips,
+        )(mixed, *arrived),
         0, 1,
     )
     decode_out = call(
         combine_kernel, "combine", struct((total, channels), jnp.bfloat16),
-        [SMEM] + [VMEM] * (3 + chips),
-        scratch=[f32(reach, width, channels)],
-    )(source, mixed, unit, swapped, *arrived)
+        [ANY] + [VMEM] * (3 + chips),
+        scratch=[
+            pltpu.SMEM((reach,), jnp.int32), f32(total, channels), pltpu.SemaphoreType.DMA((1,)),
+        ],
+    )(row_of, mixed, unit, swapped, *arrived)
     return prefill_out, decode_out.reshape(steps, rows, channels)
 
 

time: 63.9 us -> 61.7 us (0.966)
  Pallas kernels: 14.2 us -> 11.9 us
  waiting for transfers between devices: 2.69 us -> 3.85 us
  starting transfers between devices: 12.4 us -> 11.3 us
    pallas_call x1, Pallas kernels: 7.76 us -> 6.58 us  [local(): call(functools.partial(rest_kernel, groups=groups), 'rest', (struct((toke...]
    ppermute x4, waiting for transfers between devices: 2.69 us -> 3.85 us  [move(): return lax.ppermute(states, 'group', pairs)]
    ppermute x4, starting transfers between devices: 12.4 us -> 11.3 us  [move(): return lax.ppermute(states, 'group', pairs)]
  transfers between devices with their start and end apart: 4 -> 4, of which waited for: 2 -> 2; matrix products, arithmetic and copies ran while one was open for 0% -> 0% of each run, Pallas kernels for 12% -> 11%
where the time goes in v6:
time: 61.7 us; the launch traced here: 61.5 us
  blocking collectives  33.6 us (54%)
  Pallas kernels  11.9 us (19%)
  starting transfers between devices  11.3 us (18%)
  waiting for transfers between devices  3.85 us (6%)
  between operations  0.76 us (1%)
    all_to_all x2, blocking collectives, exchange(): return lax.all_to_all(chunks, 'tp', 0, 0).reshape(ranks * height, LANES)  33.6 us
    ppermute x4, starting transfers between devices, move(): return lax.ppermute(states, 'group', pairs)  11.3 us
    pallas_call x1, Pallas kernels, local(): call(functools.partial(rest_kernel, groups=groups), 'rest', (struct((toke...  6.58 us
    ppermute x4, waiting for transfers between devices, move(): return lax.ppermute(states, 'group', pairs)  3.85 us
    pallas_call x1, Pallas kernels, local(): call(states_kernel, 'states', (struct((2, CAP, width, channels)),) * chip...  2.25 us
    pallas_call x1, Pallas kernels, local(): call(functools.partial(project_kernel, rank=rank), 'project', flat, [ANY]...  1.53 us
    pallas_call x1, Pallas kernels, local(): call(combine_kernel, 'combine', struct((total, channels), jnp.bfloat16),...  1.5 us
  transfers between devices with their start and end apart: 4, of which 2 were waited for; matrix products, arithmetic and copies ran while one was open for 0% of the time, Pallas kernels for 11%

profile of v6, /device:TPU:1, one launch (start us, length us, event | category | flops | bytes accessed | tf_op | source)
XLA Modules:
  0.0 61.5 jit_solution(3255864445815700177)
XLA Ops:
  0.6 0.0 copy-start
  0.6 0.0 copy-start.1
  0.7 0.0 copy-start.2
  0.7 0.0 copy-start.3
  0.7 0.0 copy-start.4
  0.7 0.0 copy-start.5
  0.7 1.5 %project.1 = f32[1088,128]{1,0:T(8,128)S(1)} custom-call(bf16[544,512]{1,0:T(8,128)(2,1)} %bitcast.20, bf16[128,512]{1,0:T(8,128)(2,1)} %x_ref.1, bf16[128,512]{1,0:T(8,128)(2,1)} %bitcast.22), custom_call_target="tpu_custom_call" | custom-call | bytes 1048576 | tf_op jit(solution)/shard_map/project/pallas_call | solution.py:398
  2.2 20.4 %all_to_all.10 = f32[32,17,2,128]{3,2,1,0:T(2,128)S(1)} all-to-all(f32[32,17,2,128]{3,2,1,0:T(2,128)S(1)} %bitcast.15), channel_id=1, replica_groups=mesh['group'=8,'tp'=32] {'tp'}, dimensions={0} | all-to-all | bytes 1114112 | tf_op jit(solution)/shard_map/all_to_all | solution.py:396
  22.6 0.1 total.1
  22.7 13.3 %all_to_all.11 = f32[32,17,2,128]{3,2,1,0:T(2,128)S(1)} all-to-all(f32[32,17,2,128]{3,2,1,0:T(2,128)S(1)} %bitcast.14), channel_id=1, replica_groups=mesh['group'=8,'tp'=32] {'tp'}, dimensions={0} | all-to-all | bytes 1114112 | tf_op jit(solution)/shard_map/all_to_all | solution.py:396
  35.9 0.0 copy-done
  35.9 0.0 copy-done.1
  35.9 0.0 copy-done.2
  36.0 0.0 copy-done.3
  36.0 0.0 copy-done.4
  36.0 0.0 copy-done.5
  36.0 2.3 %states.1 = (f32[2,2,16,512]{3,2,1,0:T(8,128)S(1)}, f32[2,2,16,512]{3,2,1,0:T(8,128)S(1)}, f32[2,2,16,512]{3,2,1,0:T(8,128)S(1)}, f32[2,2,16,512]{3,2,1,0:T(8,128)S(1)}) custom-call(s32[1,8]{1,0:T(1,128)S(1)} %copy-done.4, s32[1,64]{1,0:T(1,128)S(1)} %bitcast.18, f32[1088,128]{1,0:T(8,128)S(1)} %bitcast.11, bf16[128,512]{1,0:T(8,128)(2,1)S(1)} %copy-done.1, ...), custom_call_target="tpu_custom_call" | custom-call | bytes 1048576 | tf_op jit(solution)/shard_map/states/pallas_call | solution.py:415
  38.2 3.1 %collective-permute-start = (f32[2,2,16,512]{3,2,1,0:T(8,128)S(1)}, f32[2,2,16,512]{3,2,1,0:T(8,128)S(1)}, u32[]{:S(2)}, u32[]{:S(2)}) collective-permute-start(f32[2,2,16,512]{3,2,1,0:T(8,128)S(1)} %get-tuple-element.15), channel_id=1, source_target_pairs={{0,64},{32,96},{64,128},{96,160},{128,192},{160,224},{192,0},{224,... | collective-permute-start | bytes 393224 | tf_op jit(solution)/shard_map/ppermute | solution.py:430
  41.3 4.2 %collective-permute-start.1 = (f32[2,2,16,512]{3,2,1,0:T(8,128)S(1)}, f32[2,2,16,512]{3,2,1,0:T(8,128)S(1)}, u32[]{:S(2)}, u32[]{:S(2)}) collective-permute-start(f32[2,2,16,512]{3,2,1,0:T(8,128)S(1)} %get-tuple-element.16), channel_id=1, source_target_pairs={{0,128},{32,160},{64,192},{96,224},{128,0},{160,32},{192,64},{224,... | collective-permute-start | bytes 393224 | tf_op jit(solution)/shard_map/ppermute | solution.py:430
  45.5 2.4 %collective-permute-start.2 = (f32[2,2,16,512]{3,2,1,0:T(8,128)S(1)}, f32[2,2,16,512]{3,2,1,0:T(8,128)S(1)}, u32[]{:S(2)}, u32[]{:S(2)}) collective-permute-start(f32[2,2,16,512]{3,2,1,0:T(8,128)S(1)} %get-tuple-element.17), channel_id=1, source_target_pairs={{0,192},{32,224},{64,0},{96,32},{128,64},{160,96},{192,128},{224,1... | collective-permute-start | bytes 393224 | tf_op jit(solution)/shard_map/ppermute | solution.py:430
  47.9 6.6 %rest.1 = (bf16[128,512]{1,0:T(8,128)(2,1)}, f32[128,512]{1,0:T(8,128)S(1)}, f32[17,4,16,512]{3,2,1,0:T(8,128)S(1)}, s32[16]{0:T(128)S(1)}) custom-call(f32[1088,128]{1,0:T(8,128)S(1)} %bitcast.12, bf16[512,512]{1,0:T(8,128)(2,1)S(1)} %copy-done, f32[16,512]{1,0:T(8,128)S(1)} %copy-done.2, f32[1,512]{1,0:T(1,128)S(1)} %bitcast.17, ...), custom_call_target="tpu_custom_call" | custom-call | flops 8000000000 | bytes 1048576 | tf_op jit(solution)/shard_map/rest/pallas_call | solution.py:435
  54.5 0.0 collective-permute-done.refs_1_.rest_1_
  54.5 0.0 collective-permute-done.1.refs_2_.rest_2_
  54.5 2.7 %collective-permute-done.2.refs_3_.rest_3_ = f32[2,2,16,512]{3,2,1,0:T(8,128)S(1)} collective-permute-done((f32[2,2,16,512]{3,2,1,0:T(8,128)S(1)}, f32[2,2,16,512]{3,2,1,0:T(8,128)S(1)}, u32[]{:S(2)}, u32[]{:S(2)}) %collective-permute-start.2) | collective-permute-done | bytes 131104 | tf_op jit(solution)/shard_map/ppermute | solution.py:430
  57.2 1.6 %collective-permute-start.3 = (f32[4,2,16,512]{3,2,1,0:T(8,128)S(1)}, f32[4,2,16,512]{3,2,1,0:T(8,128)S(1)}, u32[]{:S(2)}, u32[]{:S(2)}) collective-permute-start(f32[4,2,16,512]{3,2,1,0:T(8,128)S(1)} %pass_on.1), channel_id=1, source_target_pairs={{0,32},{32,0},{64,96},{96,64},{128,160},{160,128},{192,224},{224,1... | collective-permute-start | bytes 786440 | tf_op jit(solution)/shard_map/ppermute | solution.py:430
  58.8 1.2 %collective-permute-done.3.swapped_ref = f32[4,2,16,512]{3,2,1,0:T(8,128)S(1)} collective-permute-done((f32[4,2,16,512]{3,2,1,0:T(8,128)S(1)}, f32[4,2,16,512]{3,2,1,0:T(8,128)S(1)}, u32[]{:S(2)}, u32[]{:S(2)}) %collective-permute-start.3) | collective-permute-done | bytes 262176 | tf_op jit(solution)/shard_map/ppermute | solution.py:430
  60.0 1.5 %combine.1 = bf16[128,512]{1,0:T(8,128)(2,1)} custom-call(s32[16]{0:T(128)S(1)} %get-tuple-element.11.row_any, f32[128,512]{1,0:T(8,128)S(1)} %get-tuple-element.12.mixed_ref, f32[17,4,16,512]{3,2,1,0:T(8,128)S(1)} %get-tuple-element.13.unit_ref, f32[4,2,16,512]{3,2,1,0:T(8,128)S(1)} %collective-permute-done.3.swapped_ref, ...), custom_call_target="tpu_custom_call" | custom-call | bytes 1048576 | tf_op jit(solution)/shard_map/combine/pallas_call | solution.py:463
  (1 shorter events, 0.0 us)
Async XLA Ops:
  0.6 35.3 %copy-start = (bf16[512,512]{1,0:T(8,128)(2,1)S(1)}, bf16[512,512]{1,0:T(8,128)(2,1)}, u32[]{:S(2)}) copy-start(bf16[512,512]{1,0:T(8,128)(2,1)} %weight_ref.3) | copy-start | bytes 1572868
  0.6 35.3 %copy-start.1 = (bf16[128,512]{1,0:T(8,128)(2,1)S(1)}, bf16[128,512]{1,0:T(8,128)(2,1)}, u32[]{:S(2)}) copy-start(bf16[128,512]{1,0:T(8,128)(2,1)} %x_ref.1) | copy-start | bytes 393220
  0.7 35.3 %copy-start.2 = (f32[16,512]{1,0:T(8,128)S(1)}, f32[16,512]{1,0:T(8,128)}, u32[]{:S(2)}) copy-start(f32[16,512]{1,0:T(8,128)} %alog_ref.3) | copy-start | bytes 98308
  0.7 35.3 %copy-start.3 = (f32[512]{0:T(512)S(1)}, f32[512]{0:T(512)}, u32[]{:S(2)}) copy-start(f32[512]{0:T(512)} %param.21) | copy-start | bytes 6148
  0.7 35.3 %copy-start.4 = (s32[1,8]{1,0:T(1,128)S(1)}, s32[1,8]{1,0:T(1,128)}, u32[]{:S(2)}) copy-start(s32[1,8]{1,0:T(1,128)} %lengths_any.3) | copy-start | bytes 100
  0.7 35.3 %copy-start.5 = (s32[64,1]{0,1:T(1,128)S(1)}, s32[64,1]{0,1:T(1,128)}, u32[]{:S(2)}) copy-start(s32[64,1]{0,1:T(1,128)} %param.15) | copy-start | bytes 772
  38.2 16.3 %collective-permute-start = (f32[2,2,16,512]{3,2,1,0:T(8,128)S(1)}, f32[2,2,16,512]{3,2,1,0:T(8,128)S(1)}, u32[]{:S(2)}, u32[]{:S(2)}) collective-permute-start(f32[2,2,16,512]{3,2,1,0:T(8,128)S(1)} %get-tuple-element.15), channel_id=1, source_target_pairs={{0,64},{32,96},{64,128},{96,160},{128,192},{160,224},{192,0},{224,... | collective-permute-start | bytes 393224 | tf_op jit(solution)/shard_map/ppermute | solution.py:430
  41.3 13.2 %collective-permute-start.1 = (f32[2,2,16,512]{3,2,1,0:T(8,128)S(1)}, f32[2,2,16,512]{3,2,1,0:T(8,128)S(1)}, u32[]{:S(2)}, u32[]{:S(2)}) collective-permute-start(f32[2,2,16,512]{3,2,1,0:T(8,128)S(1)} %get-tuple-element.16), channel_id=1, source_target_pairs={{0,128},{32,160},{64,192},{96,224},{128,0},{160,32},{192,64},{224,... | collective-permute-start | bytes 393224 | tf_op jit(solution)/shard_map/ppermute | solution.py:430
  45.5 11.7 %collective-permute-start.2 = (f32[2,2,16,512]{3,2,1,0:T(8,128)S(1)}, f32[2,2,16,512]{3,2,1,0:T(8,128)S(1)}, u32[]{:S(2)}, u32[]{:S(2)}) collective-permute-start(f32[2,2,16,512]{3,2,1,0:T(8,128)S(1)} %get-tuple-element.17), channel_id=1, source_target_pairs={{0,192},{32,224},{64,0},{96,32},{128,64},{160,96},{192,128},{224,1... | collective-permute-start | bytes 393224 | tf_op jit(solution)/shard_map/ppermute | solution.py:430
  57.2 2.8 %collective-permute-start.3 = (f32[4,2,16,512]{3,2,1,0:T(8,128)S(1)}, f32[4,2,16,512]{3,2,1,0:T(8,128)S(1)}, u32[]{:S(2)}, u32[]{:S(2)}) collective-permute-start(f32[4,2,16,512]{3,2,1,0:T(8,128)S(1)} %pass_on.1), channel_id=1, source_target_pairs={{0,32},{32,0},{64,96},{96,64},{128,160},{160,128},{192,224},{224,1... | collective-permute-start | bytes 786440 | tf_op jit(solution)/shard_map/ppermute | solution.py:430

commit v7 on v6

--- a/solution.py
+++ b/solution.py
@@ -213,12 +213,21 @@
     lax.fori_loop(0, tokens // 8, block, (zero,) * len(tiles), unroll=16)
 
 
+def places_on(source, dest, chips):
+    on = dest // 2 - source // 2 + chips
+    return lax.rem(jnp.where(lax.rem(source, 2) == 0, on, 2 * chips - on), chips)
+
+
+def far_first(chips):
+    return sorted(range(chips), key=lambda ahead: -min(ahead, chips - ahead))
+
+
 def states_kernel(
     lengths_any, routes_any, proj_ref, x_ref, weight_ref, bias_ref, alog_ref,
     *rest,
 ):
-    send_refs, rest = rest[:-9], rest[-9:]
-    lengths_ref, routes_ref, size_ref, force_ref, vec_ref, rates_ref, hist_ref, send_ref, sems = rest
+    size_ref, force_ref, *send_refs = rest[:-7]
+    lengths_ref, routes_ref, vec_ref, rates_ref, hist_ref, send_ref, sems = rest[-7:]
     tables = fetch((lengths_any, routes_any), (lengths_ref, routes_ref), sems)
     chips = len(send_refs)
     requests = lengths_ref.shape[1]
@@ -234,29 +243,24 @@
         lane = jnp.int32(0)
         for j in range(k):
             lane = lane + (dests[j] == dests[k]).astype(jnp.int32)
-        ahead = lax.rem(dests[k] // 2 - group // 2 + chips, chips)
+        ahead = places_on(group, dests[k], chips)
         other = lax.rem(dests[k] + group, 2)
         send_ref[ahead, other, lane] = hist_ref[ends[k]]
-    for chip in range(chips):
-        send_refs[chip][...] = send_ref[chip]
+    for ref, ahead in zip(send_refs, far_first(chips)):
+        ref[...] = send_ref[ahead]
 
 
 def rest_kernel(
     proj_ref, weight_ref, alog_ref, bias_ref, prefill_x_ref,
-    lengths_any, routes_any, prefill_gate_hbm, skip_hbm, decode_x_hbm, decode_gate_hbm, state_hbm,
+    prefill_size_ref, prefill_force_ref,
+    routes_any, prefill_gate_hbm, skip_hbm, decode_x_hbm, decode_gate_hbm, state_hbm,
     out_ref, mixed_ref, unit_ref, row_ref,
-    lengths_ref, routes_ref, prefill_gate_ref, skip_ref, decode_x_ref, decode_gate_ref, state_ref,
+    routes_ref, prefill_gate_ref, skip_ref, decode_x_ref, decode_gate_ref, state_ref,
     source_ref, size_ref, force_ref, act_ref, sum_ref, part_ref, vec_ref, rates_ref, sems, *, groups,
 ):
     copies = fetch(
-        (
-            lengths_any, routes_any, prefill_gate_hbm, skip_hbm, decode_x_hbm, decode_gate_hbm,
-            state_hbm,
-        ),
-        (
-            lengths_ref, routes_ref, prefill_gate_ref, skip_ref, decode_x_ref, decode_gate_ref,
-            state_ref,
-        ),
+        (routes_any, prefill_gate_hbm, skip_hbm, decode_x_hbm, decode_gate_hbm, state_hbm),
+        (routes_ref, prefill_gate_ref, skip_ref, decode_x_ref, decode_gate_ref, state_ref),
         sems,
     )
     total, channels = decode_x_ref.shape
@@ -266,20 +270,18 @@
     tiles = tiles_of(channels)
     rank = weight_ref.shape[0]
     count = vec_ref.shape[0]
-    requests = lengths_ref.shape[1]
+    requests = routes_ref.shape[1] // groups
     me = lax.axis_index("group")
 
-    prepare_scan(
-        copies[0], lengths_ref, proj_ref, prefill_x_ref, weight_ref, bias_ref, alog_ref, size_ref,
-        force_ref, vec_ref, rates_ref,
-    )
-    scan(size_ref, force_ref, vec_ref, rates_ref, sum_ref, part_ref, None)
+    rates_ref[...] = -LOG2E * jnp.exp(alog_ref[...])
+    vec_ref[...] = proj_ref[vector_rows(rank, count, 0), :]
+    scan(prefill_size_ref, prefill_force_ref, vec_ref, rates_ref, sum_ref, part_ref, None)
+    copies[1].wait()
     copies[2].wait()
-    copies[3].wait()
     mixed = sum_ref[...] + skip_ref[...] * prefill_x_ref[...].astype(jnp.float32)
     out_ref[...] = (mixed * silu(prefill_gate_ref[...].astype(jnp.float32))).astype(out_ref.dtype)
 
-    copies[1].wait()
+    copies[0].wait()
     for n in range(reach):
         source_ref[n] = reach
         row_ref[n] = -1
@@ -291,7 +293,7 @@
 
             @pl.when(ours)
             def _(g=g, slot=slot, lane=lane):
-                behind = lax.rem(me // 2 - g // 2 + groups // 2, groups // 2)
+                behind = places_on(jnp.int32(g), me, groups // 2)
                 source = (behind * 2 + lax.rem(me + g, 2)) * CAP + lane
                 source_ref[slot] = source
                 row_ref[source] = slot
@@ -299,15 +301,15 @@
             slot = slot + ours.astype(jnp.int32)
             lane = lane + ours.astype(jnp.int32)
 
+    copies[3].wait()
     copies[4].wait()
-    copies[5].wait()
     size = step_sizes(low_part(proj_ref, rank, count // 2, 1), weight_ref, bias_ref)
     values = decode_x_ref[...].astype(jnp.float32)
     size_ref[...] = size
     force_ref[...] = size * values
     vec_ref[...] = proj_ref[vector_rows(rank, count, 1), :]
     act_ref[...] = silu(decode_gate_ref[...].astype(jnp.float32))
-    copies[6].wait()
+    copies[5].wait()
 
     def block(b, carry, units):
         base = pl.multiple_of(b * 8, 8)
@@ -346,8 +348,8 @@
 
 
 def pass_on_kernel(mixed_ref, *refs):
-    for i, ref in enumerate(refs[:-1]):
-        refs[-1][i] = ref[1]
+    for ref, ahead in zip(refs[:-1], far_first(len(refs) - 1)):
+        refs[-1][ahead] = ref[1]
 
 
 def combine_kernel(row_any, mixed_ref, unit_ref, swapped_ref, *rest):
@@ -357,16 +359,17 @@
     rows = mixed_ref.shape[0] // steps
     sum_ref[...] = mixed_ref[...]
     added = []
-    for i, ref in enumerate(here_refs):
+    for ref, ahead in zip(here_refs, far_first(len(here_refs))):
         for c in range(2 * CAP):
-            state = ref[0, c] if c < CAP else swapped_ref[i, c - CAP]
+            state = ref[0, c] if c < CAP else swapped_ref[ahead, c - CAP]
             for s in range(steps):
-                terms = unit_ref[2 * CAP * i + c, s] * state
-                added.append(jnp.sum(terms, axis=0, keepdims=True))
+                terms = unit_ref[2 * CAP * ahead + c, s] * state
+                term = jnp.sum(terms, axis=0, keepdims=True)
+                added.append((2 * CAP * ahead + c, s, term))
     table.wait()
-    for i, term in enumerate(added):
-        row = row_ref[i // steps]
-        at = pl.ds(i % steps * rows + jnp.maximum(row, 0), 1)
+    for slot, s, term in added:
+        row = row_ref[slot]
+        at = pl.ds(s * rows + jnp.maximum(row, 0), 1)
         sum_ref[at, :] = sum_ref[at, :] + jnp.where(row >= 0, term, 0.0)
     out_ref[...] = sum_ref[...].astype(out_ref.dtype)
 
@@ -408,16 +411,15 @@
     proj = exchange(copies)
 
     tables = [pltpu.SMEM(lengths.shape, jnp.int32), pltpu.SMEM(routes.shape, jnp.int32)]
-    scan_scratch = [
-        f32(tokens, channels), f32(tokens, channels), f32(2 * width, tokens), f32(width, channels)
-    ]
     chips = groups // 2
-    send = call(
-        states_kernel, "states", (struct((2, CAP, width, channels)),) * chips,
+    size, force, *send = call(
+        states_kernel, "states",
+        (struct((tokens, channels)),) * 2 + (struct((2, CAP, width, channels)),) * chips,
         [ANY, ANY] + [VMEM] * 5,
-        out_specs=(VMEM,) * chips,
-        scratch=tables + scan_scratch
+        out_specs=(VMEM,) * (2 + chips),
+        scratch=tables
         + [
+            f32(2 * width, tokens), f32(width, channels),
             f32(tokens, width, channels), f32(chips, 2, CAP, width, channels),
             pltpu.SemaphoreType.DMA((2,)),
         ],
@@ -425,32 +427,32 @@
 
     def move(states, ahead, other):
         pairs = [
-            (g, (g // 2 + ahead) % chips * 2 + (g + other) % 2) for g in range(groups)
+            (g, (g // 2 + (ahead if g % 2 == 0 else -ahead)) % chips * 2 + (g + other) % 2)
+            for g in range(groups)
         ]
         return lax.ppermute(states, "group", pairs)
 
-    arrived = [send[0]] + [None] * (chips - 1)
-    for ahead in sorted(range(1, chips), key=lambda d: min(d, chips - d)):
-        arrived[ahead] = move(send[ahead], ahead, 0)
+    arrived = [move(states, ahead, 0) for states, ahead in zip(send, far_first(chips)) if ahead]
+    arrived.append(send[-1])
     prefill_out, mixed, unit, row_of = call(
         functools.partial(rest_kernel, groups=groups), "rest",
         (
             struct((tokens, channels), jnp.bfloat16), struct((total, channels)),
             struct((reach + 1, steps, width, channels)), struct((reach,), jnp.int32),
         ),
-        [VMEM] * 5 + [ANY] * 7,
+        [VMEM] * 7 + [ANY] * 6,
         out_specs=(VMEM, VMEM, VMEM, SMEM),
-        scratch=tables + [
+        scratch=tables[1:] + [
             bf16(tokens, channels), f32(1, channels), bf16(total, channels),
             bf16(total, channels), f32(rows, width, channels),
             pltpu.SMEM((reach,), jnp.int32),
             f32(total, channels), f32(total, channels), f32(total, channels),
             f32(total, channels), f32(channels // LANES, steps * 64, LANES),
-            f32(2 * width, total), f32(width, channels), pltpu.SemaphoreType.DMA((7,)),
+            f32(2 * width, total), f32(width, channels), pltpu.SemaphoreType.DMA((6,)),
         ],
         flops=8 * 10**9,
     )(
-        proj, dt_weight, a_log, bias, prefill_x, lengths, routes,
+        proj, dt_weight, a_log, bias, prefill_x, size, force, routes,
         *stay(prefill_gate, skip, decode_flat, gate_flat, cached_state),
     )
     swapped = move(

time: 61.7 us -> 61.2 us (level)
  waiting for transfers between devices: 3.85 us -> 3.13 us
  starting transfers between devices: 11.3 us -> 12 us
    ppermute x4, starting transfers between devices: 11.3 us -> 12 us  [move(): return lax.ppermute(states, 'group', pairs)]
    ppermute x4, waiting for transfers between devices: 3.85 us -> 3.13 us  [move(): return lax.ppermute(states, 'group', pairs)]
  transfers between devices with their start and end apart: 4 -> 4, of which waited for: 2 -> 3; matrix products, arithmetic and copies ran while one was open for 0% -> 0% of each run, Pallas kernels for 11% -> 10%
where the time goes in v7:
time: 61.2 us; the launch traced here: 61 us
  blocking collectives  33.6 us (55%)
  starting transfers between devices  12 us (20%)
  Pallas kernels  11.4 us (19%)
  waiting for transfers between devices  3.13 us (5%)
  between operations  0.75 us (1%)
    all_to_all x2, blocking collectives, exchange(): return lax.all_to_all(chunks, 'tp', 0, 0).reshape(ranks * height, LANES)  33.6 us
    ppermute x4, starting transfers between devices, move(): return lax.ppermute(states, 'group', pairs)  12 us
    pallas_call x1, Pallas kernels, local(): call(functools.partial(rest_kernel, groups=groups), 'rest', (struct((toke...  6.09 us
    ppermute x4, waiting for transfers between devices, move(): return lax.ppermute(states, 'group', pairs)  3.13 us
    pallas_call x1, Pallas kernels, local(): call(states_kernel, 'states', (struct((tokens, channels)),) * 2 + (struct...  2.22 us
    pallas_call x1, Pallas kernels, local(): call(functools.partial(project_kernel, rank=rank), 'project', flat, [ANY]...  1.53 us
    pallas_call x1, Pallas kernels, local(): call(combine_kernel, 'combine', struct((total, channels), jnp.bfloat16),...  1.5 us
  transfers between devices with their start and end apart: 4, of which 3 were waited for; matrix products, arithmetic and copies ran while one was open for 0% of the time, Pallas kernels for 10%

profile of v7, /device:TPU:1, one launch (start us, length us, event | category | flops | bytes accessed | tf_op | source)
XLA Modules:
  0.0 61.0 jit_solution(15213003546664350166)
XLA Ops:
  0.6 0.0 copy-start
  0.6 0.0 copy-start.1
  0.7 0.0 copy-start.2
  0.7 0.0 copy-start.3
  0.7 0.0 copy-start.4
  0.7 0.0 copy-start.5
  0.7 1.5 %project.1 = f32[1088,128]{1,0:T(8,128)S(1)} custom-call(bf16[544,512]{1,0:T(8,128)(2,1)} %bitcast.20, bf16[128,512]{1,0:T(8,128)(2,1)} %prefill_x_ref.1, bf16[128,512]{1,0:T(8,128)(2,1)} %bitcast.22), custom_call_target="tpu_custom_call" | custom-call | bytes 1048576 | tf_op jit(solution)/shard_map/project/pallas_call | solution.py:401
  2.2 20.4 %all_to_all.10 = f32[32,17,2,128]{3,2,1,0:T(2,128)S(1)} all-to-all(f32[32,17,2,128]{3,2,1,0:T(2,128)S(1)} %bitcast.15), channel_id=1, replica_groups=mesh['group'=8,'tp'=32] {'tp'}, dimensions={0} | all-to-all | bytes 1114112 | tf_op jit(solution)/shard_map/all_to_all | solution.py:399
  22.6 0.1 total.1
  22.7 13.3 %all_to_all.11 = f32[32,17,2,128]{3,2,1,0:T(2,128)S(1)} all-to-all(f32[32,17,2,128]{3,2,1,0:T(2,128)S(1)} %bitcast.14), channel_id=1, replica_groups=mesh['group'=8,'tp'=32] {'tp'}, dimensions={0} | all-to-all | bytes 1114112 | tf_op jit(solution)/shard_map/all_to_all | solution.py:399
  35.9 0.0 copy-done
  35.9 0.0 copy-done.1
  35.9 0.0 copy-done.2
  36.0 0.0 copy-done.3
  36.0 0.0 copy-done.4
  36.0 0.0 copy-done.5
  36.0 2.2 %states.1 = (f32[128,512]{1,0:T(8,128)S(1)}, f32[128,512]{1,0:T(8,128)S(1)}, f32[2,2,16,512]{3,2,1,0:T(8,128)S(1)}, f32[2,2,16,512]{3,2,1,0:T(8,128)S(1)}, f32[2...) custom-call(s32[1,8]{1,0:T(1,128)S(1)} %copy-done.4, s32[1,64]{1,0:T(1,128)S(1)} %bitcast.18, ...), custom_call_target="tpu_custom_call" | custom-call | bytes 1048576 | tf_op jit(solution)/shard_map/states/pallas_call | solution.py:415
  38.2 6.1 %collective-permute-start = (f32[2,2,16,512]{3,2,1,0:T(8,128)S(1)}, f32[2,2,16,512]{3,2,1,0:T(8,128)S(1)}, u32[]{:S(2)}, u32[]{:S(2)}) collective-permute-start(f32[2,2,16,512]{3,2,1,0:T(8,128)S(1)} %get-tuple-element.18), channel_id=1, source_target_pairs={{0,128},{32,160},{64,192},{96,224},{128,0},{160,32},{192,64},{224,... | collective-permute-start | bytes 393224 | tf_op jit(solution)/shard_map/ppermute | solution.py:433
  44.3 0.3 collective-permute-start.1
  44.6 2.1 %collective-permute-start.2 = (f32[2,2,16,512]{3,2,1,0:T(8,128)S(1)}, f32[2,2,16,512]{3,2,1,0:T(8,128)S(1)}, u32[]{:S(2)}, u32[]{:S(2)}) collective-permute-start(f32[2,2,16,512]{3,2,1,0:T(8,128)S(1)} %get-tuple-element.20), channel_id=1, source_target_pairs={{0,192},{32,96},{64,0},{96,160},{128,64},{160,224},{192,128},{224,... | collective-permute-start | bytes 393224 | tf_op jit(solution)/shard_map/ppermute | solution.py:433
  46.7 6.1 %rest.1 = (bf16[128,512]{1,0:T(8,128)(2,1)}, f32[128,512]{1,0:T(8,128)S(1)}, f32[17,4,16,512]{3,2,1,0:T(8,128)S(1)}, s32[16]{0:T(128)S(1)}) custom-call(f32[1088,128]{1,0:T(8,128)S(1)} %bitcast.12, bf16[512,512]{1,0:T(8,128)(2,1)S(1)} %copy-done, f32[16,512]{1,0:T(8,128)S(1)} %copy-done.2, f32[1,512]{1,0:T(1,128)S(1)} %bitcast.17, ...), custom_call_target="tpu_custom_call" | custom-call | flops 8000000000 | bytes 1048576 | tf_op jit(solution)/shard_map/rest/pallas_call | solution.py:437
  52.8 0.0 collective-permute-done.refs_0_.rest_0_
  52.8 1.3 %collective-permute-done.1.refs_1_.rest_1_ = f32[2,2,16,512]{3,2,1,0:T(8,128)S(1)} collective-permute-done((f32[2,2,16,512]{3,2,1,0:T(8,128)S(1)}, f32[2,2,16,512]{3,2,1,0:T(8,128)S(1)}, u32[]{:S(2)}, u32[]{:S(2)}) %collective-permute-start.1) | collective-permute-done | bytes 131104 | tf_op jit(solution)/shard_map/ppermute | solution.py:433
  54.1 0.7 %collective-permute-done.2.refs_2_.rest_2_ = f32[2,2,16,512]{3,2,1,0:T(8,128)S(1)} collective-permute-done((f32[2,2,16,512]{3,2,1,0:T(8,128)S(1)}, f32[2,2,16,512]{3,2,1,0:T(8,128)S(1)}, u32[]{:S(2)}, u32[]{:S(2)}) %collective-permute-start.2) | collective-permute-done | bytes 131104 | tf_op jit(solution)/shard_map/ppermute | solution.py:433
  54.8 3.6 %collective-permute-start.3 = (f32[4,2,16,512]{3,2,1,0:T(8,128)S(1)}, f32[4,2,16,512]{3,2,1,0:T(8,128)S(1)}, u32[]{:S(2)}, u32[]{:S(2)}) collective-permute-start(f32[4,2,16,512]{3,2,1,0:T(8,128)S(1)} %pass_on.1), channel_id=1, source_target_pairs={{0,32},{32,0},{64,96},{96,64},{128,160},{160,128},{192,224},{224,1... | collective-permute-start | bytes 786440 | tf_op jit(solution)/shard_map/ppermute | solution.py:433
  58.3 1.2 %collective-permute-done.3.swapped_ref = f32[4,2,16,512]{3,2,1,0:T(8,128)S(1)} collective-permute-done((f32[4,2,16,512]{3,2,1,0:T(8,128)S(1)}, f32[4,2,16,512]{3,2,1,0:T(8,128)S(1)}, u32[]{:S(2)}, u32[]{:S(2)}) %collective-permute-start.3) | collective-permute-done | bytes 262176 | tf_op jit(solution)/shard_map/ppermute | solution.py:433
  59.5 1.5 %combine.1 = bf16[128,512]{1,0:T(8,128)(2,1)} custom-call(s32[16]{0:T(128)S(1)} %get-tuple-element.15.row_any, f32[128,512]{1,0:T(8,128)S(1)} %get-tuple-element.16.mixed_ref, f32[17,4,16,512]{3,2,1,0:T(8,128)S(1)} %get-tuple-element.17.unit_ref, f32[4,2,16,512]{3,2,1,0:T(8,128)S(1)} %collective-permute-done.3.swapped_ref, ...), custom_call_target="tpu_custom_call" | custom-call | bytes 1048576 | tf_op jit(solution)/shard_map/combine/pallas_call | solution.py:465
  (1 shorter events, 0.0 us)
Async XLA Ops:
  0.6 35.3 %copy-start = (bf16[512,512]{1,0:T(8,128)(2,1)S(1)}, bf16[512,512]{1,0:T(8,128)(2,1)}, u32[]{:S(2)}) copy-start(bf16[512,512]{1,0:T(8,128)(2,1)} %weight_ref.3) | copy-start | bytes 1572868
  0.6 35.3 %copy-start.1 = (bf16[128,512]{1,0:T(8,128)(2,1)S(1)}, bf16[128,512]{1,0:T(8,128)(2,1)}, u32[]{:S(2)}) copy-start(bf16[128,512]{1,0:T(8,128)(2,1)} %prefill_x_ref.1) | copy-start | bytes 393220
  0.7 35.3 %copy-start.2 = (f32[16,512]{1,0:T(8,128)S(1)}, f32[16,512]{1,0:T(8,128)}, u32[]{:S(2)}) copy-start(f32[16,512]{1,0:T(8,128)} %alog_ref.3) | copy-start | bytes 98308
  0.7 35.3 %copy-start.3 = (f32[512]{0:T(512)S(1)}, f32[512]{0:T(512)}, u32[]{:S(2)}) copy-start(f32[512]{0:T(512)} %param.21) | copy-start | bytes 6148
  0.7 35.3 %copy-start.4 = (s32[1,8]{1,0:T(1,128)S(1)}, s32[1,8]{1,0:T(1,128)}, u32[]{:S(2)}) copy-start(s32[1,8]{1,0:T(1,128)} %lengths_any.1) | copy-start | bytes 100
  0.7 35.3 %copy-start.5 = (s32[64,1]{0,1:T(1,128)S(1)}, s32[64,1]{0,1:T(1,128)}, u32[]{:S(2)}) copy-start(s32[64,1]{0,1:T(1,128)} %param.15) | copy-start | bytes 772
  38.2 14.6 %collective-permute-start = (f32[2,2,16,512]{3,2,1,0:T(8,128)S(1)}, f32[2,2,16,512]{3,2,1,0:T(8,128)S(1)}, u32[]{:S(2)}, u32[]{:S(2)}) collective-permute-start(f32[2,2,16,512]{3,2,1,0:T(8,128)S(1)} %get-tuple-element.18), channel_id=1, source_target_pairs={{0,128},{32,160},{64,192},{96,224},{128,0},{160,32},{192,64},{224,... | collective-permute-start | bytes 393224 | tf_op jit(solution)/shard_map/ppermute | solution.py:433
  44.3 9.8 %collective-permute-start.1 = (f32[2,2,16,512]{3,2,1,0:T(8,128)S(1)}, f32[2,2,16,512]{3,2,1,0:T(8,128)S(1)}, u32[]{:S(2)}, u32[]{:S(2)}) collective-permute-start(f32[2,2,16,512]{3,2,1,0:T(8,128)S(1)} %get-tuple-element.19), channel_id=1, source_target_pairs={{0,64},{32,224},{64,128},{96,32},{128,192},{160,96},{192,0},{224,1... | collective-permute-start | bytes 393224 | tf_op jit(solution)/shard_map/ppermute | solution.py:433
  44.6 10.2 %collective-permute-start.2 = (f32[2,2,16,512]{3,2,1,0:T(8,128)S(1)}, f32[2,2,16,512]{3,2,1,0:T(8,128)S(1)}, u32[]{:S(2)}, u32[]{:S(2)}) collective-permute-start(f32[2,2,16,512]{3,2,1,0:T(8,128)S(1)} %get-tuple-element.20), channel_id=1, source_target_pairs={{0,192},{32,96},{64,0},{96,160},{128,64},{160,224},{192,128},{224,... | collective-permute-start | bytes 393224 | tf_op jit(solution)/shard_map/ppermute | solution.py:433
  54.8 4.7 %collective-permute-start.3 = (f32[4,2,16,512]{3,2,1,0:T(8,128)S(1)}, f32[4,2,16,512]{3,2,1,0:T(8,128)S(1)}, u32[]{:S(2)}, u32[]{:S(2)}) collective-permute-start(f32[4,2,16,512]{3,2,1,0:T(8,128)S(1)} %pass_on.1), channel_id=1, source_target_pairs={{0,32},{32,0},{64,96},{96,64},{128,160},{160,128},{192,224},{224,1... | collective-permute-start | bytes 786440 | tf_op jit(solution)/shard_map/ppermute | solution.py:433

commit v8 on v7

--- a/solution.py
+++ b/solution.py
@@ -94,7 +94,9 @@
     *, rank,
 ):
     copies = fetch(
-        (weight_hbm, prefill_hbm, decode_hbm), (weight_ref, prefill_ref, decode_ref), sems
+        (weight_hbm.at[: rank // 2], weight_hbm.at[rank // 2 :], prefill_hbm, decode_hbm),
+        (weight_ref.at[: rank // 2], weight_ref.at[rank // 2 :], prefill_ref, decode_ref),
+        sems,
     )
     count = weight_ref.shape[0] - rank
     for copy in copies:
@@ -402,7 +404,7 @@
         functools.partial(project_kernel, rank=rank), "project", flat, [ANY] * 3,
         scratch=[
             bf16(columns, channels), bf16(tokens, channels), bf16(total, channels),
-            pltpu.SemaphoreType.DMA((3,)),
+            pltpu.SemaphoreType.DMA((4,)),
         ],
     )(*stay(xproj_weight.T, prefill_x, decode_flat))
     copies = call(functools.partial(total_kernel, ranks=ranks), "total", flat, [VMEM])(

time: 61.2 us -> 61.2 us (level)
  no operation moved by 1% of the time
where the time goes in v8:
time: 61.2 us; the launch traced here: 61 us
  blocking collectives  33.6 us (55%)
  starting transfers between devices  12 us (20%)
  Pallas kernels  11.4 us (19%)
  waiting for transfers between devices  3.18 us (5%)
  between operations  0.75 us (1%)
    all_to_all x2, blocking collectives, exchange(): return lax.all_to_all(chunks, 'tp', 0, 0).reshape(ranks * height, LANES)  33.6 us
    ppermute x4, starting transfers between devices, move(): return lax.ppermute(states, 'group', pairs)  12 us
    pallas_call x1, Pallas kernels, local(): call(functools.partial(rest_kernel, groups=groups), 'rest', (struct((toke...  6.08 us
    ppermute x4, waiting for transfers between devices, move(): return lax.ppermute(states, 'group', pairs)  3.18 us
    pallas_call x1, Pallas kernels, local(): call(states_kernel, 'states', (struct((tokens, channels)),) * 2 + (struct...  2.23 us
    pallas_call x1, Pallas kernels, local(): call(functools.partial(project_kernel, rank=rank), 'project', flat, [ANY]...  1.54 us
    pallas_call x1, Pallas kernels, local(): call(combine_kernel, 'combine', struct((total, channels), jnp.bfloat16),...  1.5 us
  transfers between devices with their start and end apart: 4, of which 3 were waited for; matrix products, arithmetic and copies ran while one was open for 0% of the time, Pallas kernels for 10%

profile of v8, /device:TPU:1, one launch (start us, length us, event | category | flops | bytes accessed | tf_op | source)
XLA Modules:
  0.0 61.0 jit_solution(14356445505218241895)
XLA Ops:
  0.6 0.0 copy-start
  0.6 0.0 copy-start.1
  0.7 0.0 copy-start.2
  0.7 0.0 copy-start.3
  0.7 0.0 copy-start.4
  0.7 0.0 copy-start.5
  0.7 1.5 %project.1 = f32[1088,128]{1,0:T(8,128)S(1)} custom-call(bf16[544,512]{1,0:T(8,128)(2,1)} %bitcast.20, bf16[128,512]{1,0:T(8,128)(2,1)} %prefill_x_ref.1, bf16[128,512]{1,0:T(8,128)(2,1)} %bitcast.22), custom_call_target="tpu_custom_call" | custom-call | bytes 1048576 | tf_op jit(solution)/shard_map/project/pallas_call | solution.py:403
  2.2 20.4 %all_to_all.10 = f32[32,17,2,128]{3,2,1,0:T(2,128)S(1)} all-to-all(f32[32,17,2,128]{3,2,1,0:T(2,128)S(1)} %bitcast.15), channel_id=1, replica_groups=mesh['group'=8,'tp'=32] {'tp'}, dimensions={0} | all-to-all | bytes 1114112 | tf_op jit(solution)/shard_map/all_to_all | solution.py:401
  22.6 0.1 total.1
  22.7 13.3 %all_to_all.11 = f32[32,17,2,128]{3,2,1,0:T(2,128)S(1)} all-to-all(f32[32,17,2,128]{3,2,1,0:T(2,128)S(1)} %bitcast.14), channel_id=1, replica_groups=mesh['group'=8,'tp'=32] {'tp'}, dimensions={0} | all-to-all | bytes 1114112 | tf_op jit(solution)/shard_map/all_to_all | solution.py:401
  36.0 0.0 copy-done
  36.0 0.0 copy-done.1
  36.0 0.0 copy-done.2
  36.0 0.0 copy-done.3
  36.0 0.0 copy-done.4
  36.0 0.0 copy-done.5
  36.0 2.2 %states.1 = (f32[128,512]{1,0:T(8,128)S(1)}, f32[128,512]{1,0:T(8,128)S(1)}, f32[2,2,16,512]{3,2,1,0:T(8,128)S(1)}, f32[2,2,16,512]{3,2,1,0:T(8,128)S(1)}, f32[2...) custom-call(s32[1,8]{1,0:T(1,128)S(1)} %copy-done.4, s32[1,64]{1,0:T(1,128)S(1)} %bitcast.18, ...), custom_call_target="tpu_custom_call" | custom-call | bytes 1048576 | tf_op jit(solution)/shard_map/states/pallas_call | solution.py:417
  38.2 6.1 %collective-permute-start = (f32[2,2,16,512]{3,2,1,0:T(8,128)S(1)}, f32[2,2,16,512]{3,2,1,0:T(8,128)S(1)}, u32[]{:S(2)}, u32[]{:S(2)}) collective-permute-start(f32[2,2,16,512]{3,2,1,0:T(8,128)S(1)} %get-tuple-element.18), channel_id=1, source_target_pairs={{0,128},{32,160},{64,192},{96,224},{128,0},{160,32},{192,64},{224,... | collective-permute-start | bytes 393224 | tf_op jit(solution)/shard_map/ppermute | solution.py:435
  44.3 0.3 collective-permute-start.1
  44.6 2.1 %collective-permute-start.2 = (f32[2,2,16,512]{3,2,1,0:T(8,128)S(1)}, f32[2,2,16,512]{3,2,1,0:T(8,128)S(1)}, u32[]{:S(2)}, u32[]{:S(2)}) collective-permute-start(f32[2,2,16,512]{3,2,1,0:T(8,128)S(1)} %get-tuple-element.20), channel_id=1, source_target_pairs={{0,192},{32,96},{64,0},{96,160},{128,64},{160,224},{192,128},{224,... | collective-permute-start | bytes 393224 | tf_op jit(solution)/shard_map/ppermute | solution.py:435
  46.7 6.1 %rest.1 = (bf16[128,512]{1,0:T(8,128)(2,1)}, f32[128,512]{1,0:T(8,128)S(1)}, f32[17,4,16,512]{3,2,1,0:T(8,128)S(1)}, s32[16]{0:T(128)S(1)}) custom-call(f32[1088,128]{1,0:T(8,128)S(1)} %bitcast.12, bf16[512,512]{1,0:T(8,128)(2,1)S(1)} %copy-done, f32[16,512]{1,0:T(8,128)S(1)} %copy-done.2, f32[1,512]{1,0:T(1,128)S(1)} %bitcast.17, ...), custom_call_target="tpu_custom_call" | custom-call | flops 8000000000 | bytes 1048576 | tf_op jit(solution)/shard_map/rest/pallas_call | solution.py:439
  52.8 0.0 collective-permute-done.refs_0_.rest_0_
  52.8 1.3 %collective-permute-done.1.refs_1_.rest_1_ = f32[2,2,16,512]{3,2,1,0:T(8,128)S(1)} collective-permute-done((f32[2,2,16,512]{3,2,1,0:T(8,128)S(1)}, f32[2,2,16,512]{3,2,1,0:T(8,128)S(1)}, u32[]{:S(2)}, u32[]{:S(2)}) %collective-permute-start.1) | collective-permute-done | bytes 131104 | tf_op jit(solution)/shard_map/ppermute | solution.py:435
  54.1 0.7 %collective-permute-done.2.refs_2_.rest_2_ = f32[2,2,16,512]{3,2,1,0:T(8,128)S(1)} collective-permute-done((f32[2,2,16,512]{3,2,1,0:T(8,128)S(1)}, f32[2,2,16,512]{3,2,1,0:T(8,128)S(1)}, u32[]{:S(2)}, u32[]{:S(2)}) %collective-permute-start.2) | collective-permute-done | bytes 131104 | tf_op jit(solution)/shard_map/ppermute | solution.py:435
  54.8 3.5 %collective-permute-start.3 = (f32[4,2,16,512]{3,2,1,0:T(8,128)S(1)}, f32[4,2,16,512]{3,2,1,0:T(8,128)S(1)}, u32[]{:S(2)}, u32[]{:S(2)}) collective-permute-start(f32[4,2,16,512]{3,2,1,0:T(8,128)S(1)} %pass_on.1), channel_id=1, source_target_pairs={{0,32},{32,0},{64,96},{96,64},{128,160},{160,128},{192,224},{224,1... | collective-permute-start | bytes 786440 | tf_op jit(solution)/shard_map/ppermute | solution.py:435
  58.3 1.2 %collective-permute-done.3.swapped_ref = f32[4,2,16,512]{3,2,1,0:T(8,128)S(1)} collective-permute-done((f32[4,2,16,512]{3,2,1,0:T(8,128)S(1)}, f32[4,2,16,512]{3,2,1,0:T(8,128)S(1)}, u32[]{:S(2)}, u32[]{:S(2)}) %collective-permute-start.3) | collective-permute-done | bytes 262176 | tf_op jit(solution)/shard_map/ppermute | solution.py:435
  59.5 1.5 %combine.1 = bf16[128,512]{1,0:T(8,128)(2,1)} custom-call(s32[16]{0:T(128)S(1)} %get-tuple-element.15.row_any, f32[128,512]{1,0:T(8,128)S(1)} %get-tuple-element.16.mixed_ref, f32[17,4,16,512]{3,2,1,0:T(8,128)S(1)} %get-tuple-element.17.unit_ref, f32[4,2,16,512]{3,2,1,0:T(8,128)S(1)} %collective-permute-done.3.swapped_ref, ...), custom_call_target="tpu_custom_call" | custom-call | bytes 1048576 | tf_op jit(solution)/shard_map/combine/pallas_call | solution.py:467
  (1 shorter events, 0.0 us)
Async XLA Ops:
  0.6 35.3 %copy-start = (bf16[512,512]{1,0:T(8,128)(2,1)S(1)}, bf16[512,512]{1,0:T(8,128)(2,1)}, u32[]{:S(2)}) copy-start(bf16[512,512]{1,0:T(8,128)(2,1)} %weight_ref.3) | copy-start | bytes 1572868
  0.6 35.3 %copy-start.1 = (bf16[128,512]{1,0:T(8,128)(2,1)S(1)}, bf16[128,512]{1,0:T(8,128)(2,1)}, u32[]{:S(2)}) copy-start(bf16[128,512]{1,0:T(8,128)(2,1)} %prefill_x_ref.1) | copy-start | bytes 393220
  0.7 35.3 %copy-start.2 = (f32[16,512]{1,0:T(8,128)S(1)}, f32[16,512]{1,0:T(8,128)}, u32[]{:S(2)}) copy-start(f32[16,512]{1,0:T(8,128)} %alog_ref.3) | copy-start | bytes 98308
  0.7 35.3 %copy-start.3 = (f32[512]{0:T(512)S(1)}, f32[512]{0:T(512)}, u32[]{:S(2)}) copy-start(f32[512]{0:T(512)} %param.21) | copy-start | bytes 6148
  0.7 35.3 %copy-start.4 = (s32[1,8]{1,0:T(1,128)S(1)}, s32[1,8]{1,0:T(1,128)}, u32[]{:S(2)}) copy-start(s32[1,8]{1,0:T(1,128)} %lengths_any.1) | copy-start | bytes 100
  0.7 35.3 %copy-start.5 = (s32[64,1]{0,1:T(1,128)S(1)}, s32[64,1]{0,1:T(1,128)}, u32[]{:S(2)}) copy-start(s32[64,1]{0,1:T(1,128)} %param.15) | copy-start | bytes 772
  38.2 14.6 %collective-permute-start = (f32[2,2,16,512]{3,2,1,0:T(8,128)S(1)}, f32[2,2,16,512]{3,2,1,0:T(8,128)S(1)}, u32[]{:S(2)}, u32[]{:S(2)}) collective-permute-start(f32[2,2,16,512]{3,2,1,0:T(8,128)S(1)} %get-tuple-element.18), channel_id=1, source_target_pairs={{0,128},{32,160},{64,192},{96,224},{128,0},{160,32},{192,64},{224,... | collective-permute-start | bytes 393224 | tf_op jit(solution)/shard_map/ppermute | solution.py:435
  44.3 9.8 %collective-permute-start.1 = (f32[2,2,16,512]{3,2,1,0:T(8,128)S(1)}, f32[2,2,16,512]{3,2,1,0:T(8,128)S(1)}, u32[]{:S(2)}, u32[]{:S(2)}) collective-permute-start(f32[2,2,16,512]{3,2,1,0:T(8,128)S(1)} %get-tuple-element.19), channel_id=1, source_target_pairs={{0,64},{32,224},{64,128},{96,32},{128,192},{160,96},{192,0},{224,1... | collective-permute-start | bytes 393224 | tf_op jit(solution)/shard_map/ppermute | solution.py:435
  44.6 10.2 %collective-permute-start.2 = (f32[2,2,16,512]{3,2,1,0:T(8,128)S(1)}, f32[2,2,16,512]{3,2,1,0:T(8,128)S(1)}, u32[]{:S(2)}, u32[]{:S(2)}) collective-permute-start(f32[2,2,16,512]{3,2,1,0:T(8,128)S(1)} %get-tuple-element.20), channel_id=1, source_target_pairs={{0,192},{32,96},{64,0},{96,160},{128,64},{160,224},{192,128},{224,... | collective-permute-start | bytes 393224 | tf_op jit(solution)/shard_map/ppermute | solution.py:435
  54.8 4.7 %collective-permute-start.3 = (f32[4,2,16,512]{3,2,1,0:T(8,128)S(1)}, f32[4,2,16,512]{3,2,1,0:T(8,128)S(1)}, u32[]{:S(2)}, u32[]{:S(2)}) collective-permute-start(f32[4,2,16,512]{3,2,1,0:T(8,128)S(1)} %pass_on.1), channel_id=1, source_target_pairs={{0,32},{32,0},{64,96},{96,64},{128,160},{160,128},{192,224},{224,1... | collective-permute-start | bytes 786440 | tf_op jit(solution)/shard_map/ppermute | solution.py:435
